TPU v7x, 32 devices: a whole 2x2x4 slice. The times are simulated.
32 devices in a mesh: grp: 4 (over y, x), att: 2 (over core), dev: 4 (over z).
Axes of the slice: x: 2, y: 2, z: 4, core: 2. Of those that a mesh axis runs over, the one named last changes fastest.
Arguments:
- query: bfloat16 [8, 4, 2, 32, 1024], P(('grp', 'att'), 'dev'), parts along dimension 0, may hold values from -110 to 110
- key_cache: bfloat16 [8, 4, 2, 32, 64, 128], P(('grp', 'att'), 'dev'), parts along dimension 0, may hold values from -5.5 to 5.5
- value_cache: bfloat16 [8, 4, 2, 32, 64, 128], P(('grp', 'att'), 'dev'), parts along dimension 0, may hold values from -12 to 12
- key_new: bfloat16 [8, 4, 2, 32, 128], P(('grp', 'att'), 'dev'), parts along dimension 0, may hold values from -12 to 12
- value_new: bfloat16 [8, 4, 2, 32, 128], P(('grp', 'att'), 'dev'), parts along dimension 0, may hold values from -12 to 12
- lengths: int32 [8, 1, 2, 32], P(('grp', 'att')), parts along dimension 0, may hold values from 2 to 64, as said below
- resid: bfloat16 [8, 4, 2, 32, 1024], P(('grp', 'att'), 'dev'), parts along dimension 0, may hold values from -6 to 6
- gain: bfloat16 [4096], replicated, may hold values from 0.5 to 1.5
- w_gate: bfloat16 [4096, 14336], P(None, ('att', 'dev')), may hold values from -0.09375 to 0.09375
- w_up: bfloat16 [4096, 14336], P(None, ('att', 'dev')), may hold values from -0.09375 to 0.09375
- w_down: bfloat16 [14336, 4096], P(('att', 'dev')), may hold values from -0.0625 to 0.0625
Outputs:
- layer_out: bfloat16 [8, 4, 2, 32, 1024], P(('grp', 'att'), 'dev'), parts along dimension 0
There are 4 independent parts, one for each index of `grp`. A program takes and returns all parts, laid end to end along the dimension named above; an argument that names none is the same for every part. Nothing has to cross between parts.
Inputs may be any that keep to these rules, and one draw needn't show every extreme that they name: `lengths`: each row's cached positions; the first row of every micro-batch of every row block holds 64.
All inputs are finite; a program needn't handle non-finite values.
Results may differ from a plain program's by a relative error of at most 0.017.
Values may be sent and summed in bfloat16 or wider, within the bound.
No kernel may reach another device: no remote copies, remote signals or barrier semaphores. Data moves between devices by JAX's collectives and lax.ppermute only.
A program may use at most 128 MiB of HBM per device.

v0:
```python
import jax
import jax.numpy as jnp
from jax import lax
from jax.sharding import PartitionSpec as P

KV_HEADS = 4


def attend(queries, key_rows, value_rows, fresh_key, fresh_value, row_lengths):
    head_dim = key_rows.shape[-1]
    grouped = queries.reshape(queries.shape[:-1] + (queries.shape[-1] // head_dim, head_dim))
    score_scale = head_dim ** (-0.5)
    cached = (
        jnp.einsum("mrgc,mrtc->mrgt", grouped, key_rows, preferred_element_type=jnp.float32)
        * score_scale
    )
    fresh = (
        jnp.einsum("mrgc,mrc->mrg", grouped, fresh_key, preferred_element_type=jnp.float32)
        * score_scale
    )
    positions = lax.broadcasted_iota(jnp.int32, (1, 1, 1, key_rows.shape[-2]), 3)
    valid = positions < row_lengths[:, :, None, None]
    cached = jnp.where(valid, cached, -1e30)
    row_max = jnp.maximum(jnp.max(cached, axis=-1), fresh)
    weights = jnp.where(valid, jnp.exp(cached - row_max[..., None]), 0.0)
    own_weight = jnp.exp(fresh - row_max)
    total = jnp.sum(weights, axis=-1) + own_weight
    probs = (weights / total[..., None]).astype(jnp.bfloat16)
    own_prob = (own_weight / total).astype(jnp.bfloat16)
    attended = jnp.einsum("mrgt,mrtc->mrgc", probs, value_rows, preferred_element_type=jnp.float32)
    attended = (
        attended
        + own_prob.astype(jnp.float32)[..., None] * fresh_value.astype(jnp.float32)[:, :, None, :]
    )
    return attended.reshape(queries.shape)


def feed_forward(stream_rows, gain, w_gate, w_up, w_down):
    batches, rows, width = stream_rows.shape
    groups = lax.axis_size("att")
    devices = lax.axis_size("dev")
    blocks = devices // KV_HEADS
    gathered = lax.all_gather(stream_rows[None], ("att", "dev"), axis=0, tiled=True)
    blocked = gathered.reshape(groups, blocks, KV_HEADS, batches, rows, width)
    widened = blocked.astype(jnp.float32)
    mean_square = jnp.mean(widened * widened, axis=(2, 5), keepdims=True)
    gain_rows = gain.astype(jnp.float32).reshape(1, 1, KV_HEADS, 1, 1, width)
    normed = (widened * lax.rsqrt(mean_square + 1e-05) * gain_rows).astype(jnp.bfloat16)
    local_units = w_gate.shape[1]
    gate = jnp.einsum(
        "abkmrc,kcf->abmrf",
        normed,
        w_gate.reshape(KV_HEADS, width, local_units),
        preferred_element_type=jnp.float32,
    )
    up_part = jnp.einsum(
        "abkmrc,kcf->abmrf",
        normed,
        w_up.reshape(KV_HEADS, width, local_units),
        preferred_element_type=jnp.float32,
    )
    hidden = (jax.nn.silu(gate) * up_part).astype(jnp.bfloat16)
    partial_term = jnp.einsum(
        "abmrf,fkc->abkmrc",
        hidden,
        w_down.reshape(local_units, KV_HEADS, width),
        preferred_element_type=jnp.float32,
    )
    combined = lax.psum_scatter(
        partial_term.reshape(groups * devices, batches, rows, width).astype(jnp.bfloat16),
        ("att", "dev"),
        scatter_dimension=0,
        tiled=True,
    ).astype(jnp.float32)[0]
    return (stream_rows.astype(jnp.float32) + combined).astype(jnp.bfloat16)


def shards(
    query, key_cache, value_cache, key_new, value_new, lengths, resid, gain, w_gate, w_up, w_down
):
    block_index = lax.axis_index("dev") // KV_HEADS
    row_lengths = lax.dynamic_index_in_dim(lengths[0], block_index, 0, keepdims=False)
    queries = query[0, 0]
    key_rows = key_cache[0, 0]
    value_rows = value_cache[0, 0]
    fresh_key = key_new[0, 0]
    fresh_value = value_new[0, 0]
    residual = resid[0, 0]
    attended = attend(queries, key_rows, value_rows, fresh_key, fresh_value, row_lengths)
    stream_rows = (residual.astype(jnp.float32) + attended).astype(jnp.bfloat16)
    layer_out = feed_forward(stream_rows, gain, w_gate, w_up, w_down)
    return layer_out[None, None]


def solution(mesh):
    return jax.shard_map(
        shards,
        mesh=mesh,
        in_specs=(
            P(("grp", "att"), "dev", None, None, None),
            P(("grp", "att"), "dev", None, None, None, None),
            P(("grp", "att"), "dev", None, None, None, None),
            P(("grp", "att"), "dev", None, None, None),
            P(("grp", "att"), "dev", None, None, None),
            P(("grp", "att"), None, None, None),
            P(("grp", "att"), "dev", None, None, None),
            P(),
            P(None, ("att", "dev")),
            P(None, ("att", "dev")),
            P(("att", "dev"), None),
        ),
        out_specs=P(("grp", "att"), "dev", None, None, None),
        check_vma=False,
    )
```

profile of v0, /device:TPU:0, one launch (start us, length us, event | category | flops | bytes accessed | tf_op | source)
XLA Modules:
  0.0 121.6 jit_solution(11937403091309847127)
XLA Ops:
  6.5 0.0 copy-start
  6.5 0.0 all-gather.2.cloned.1.call-start
  6.5 0.8 iota_compare_fusion
  7.4 0.7 bitcast_convert_fusion
  8.1 0.9 copy.45
  9.0 0.9 fusion.30
  10.0 0.0 copy-start.2
  10.0 2.0 %fusion.42 = (f32[2,32,8]{2,1,0:T(8,128)S(1)}, f32[2,32,8,64]{3,2,1,0:T(8,128)S(1)}) fusion(bf16[1,1,2,32,64,128]{5,4,3,2,1,0:T(8,128)(2,1)} %param.12, pred[2,32,64]{2,1,0:T(8,128)(4,1)S(1)} %iota_compare_fusion, bf16[2,32,8,128]{3,2,1,0:T(8,128)(2,1)S(1)} %bitcast.103), kind=kOutput, calls=%fused_computation.53 | convolution fusion | flops 8486400 | bytes 1316864 | tf_op jit(solution)/shard_map/mrgc,mrtc->mrgt/dot_general | solution.py:14
  12.0 0.0 copy-start.4
  12.0 0.2 fusion.26
  12.3 0.0 copy-done
  12.3 0.5 convolution_add_fusion
  12.8 0.0 copy-done.2
  12.8 0.7 fusion.24
  13.5 0.0 all-gather.2.cloned.1.call-update
  13.5 0.0 reduce-scatter.2.cloned.1.call-start
  13.6 0.0 copy-done.4
  13.6 24.5 %reshape.115 = bf16[1792,4,1024]{2,1,0:T(4,128)(2,1)} reshape(bf16[1792,4096]{1,0:T(8,128)(2,1)} %param.21) | data formatting | bytes 29360128 | tf_op jit(solution)/shard_map/reshape | solution.py:66
  38.1 0.3 all-gather.2.cloned.1.call-done
  38.5 1.5 %multiply_reduce_fusion = f32[8,2,32]{2,1,0:T(2,128)S(1)} fusion(bf16[8,2,32,1024]{3,2,1,0:T(8,128)(2,1)} %all-gather.2.cloned.1.call-done), kind=kLoop, calls=%fused_computation.10 | loop fusion | flops 1572352 | bytes 1050624 | tf_op jit(solution)/shard_map/reduce_sum | solution.py:46
  40.0 0.0 copy-start.3
  40.0 0.0 copy-start.1
  40.0 8.6 %convolution_bitcast_fusion.1 = f32[2,2,32,1792]{3,2,1,0:T(8,128)} fusion(bf16[4,1024,1792,1,1]{2,1,0,4,3:T(8,128)(2,1)} %bitcast.98, f32[4,1024]{1,0:T(4,128)S(1)} %reshape.119, f32[2,2,32]{2,1,0:T(2,128)S(1)} %add_rsqrt_fusion, bf16[2,4,2,32,1024]{4,3,2,1,0:T(8,128)(2,1)} %bitcast.100), kind=kOutput, calls=%fused_computation.4 | convolution fusion | flops 1881145344 | bytes 16663040 | tf_op jit(solution)/shard_map/abkmrc,kcf->abmrf/dot_general | solution.py:50
  48.7 0.0 copy-done.3
  48.7 0.0 copy-done.1
  48.7 25.1 %fusion.10 = bf16[2,1,4,2,32,1024]{5,4,2,3,0,1:T(8,128)(2,1)S(1)} fusion(bf16[1792,4,1024,1,1]{2,1,0,4,3:T(4,128)(2,1)} %bitcast.97, bf16[4,1024,1792,1,1]{2,1,0,4,3:T(8,128)(2,1)} %bitcast.109, f32[2,2,32,1792]{3,2,1,0:T(8,128)} %convolution_bitcast_fusion.1, f32[4,1024]{1,0:T(4,128)S(1)} %reshape.119, f32[2,2,32]{2,1,0:T(2,128)} %copy-done.3, ...), kind=kOutput, calls=%fused_computation.12 | convolution fusion | flops 3762094080 | bytes 32391680 | tf_op jit(solution)/shard_map/abmrf,fkc->abkmrc/dot_general | solution.py:63
  73.8 1.1 copy.31
  74.9 0.0 reduce-scatter.2.cloned.1.call-update
  75.0 38.2 %reduce-scatter.2.cloned.1.call-done = bf16[1,2,32,1024]{3,2,1,0:T(8,128)(2,1)} async-done(((bf16[8,2,32,1024]{3,2,1,0:T(8,128)(2,1)}), bf16[1,2,32,1024]{3,2,1,0:T(8,128)(2,1)}) %reduce-scatter.2.cloned.1.call-update) | async-done | bytes 131088 | tf_op jit(solution)/shard_map/reduce_scatter | solution.py:69
  113.1 1.6 %fusion.25 = bf16[1,1,2,32,1024]{4,3,2,1,0:T(8,128)(2,1)} fusion(f32[1,1,2,32,1024]{4,3,2,1,0:T(8,128)S(1)} %reshape.111, bf16[1,1,2,32,1024]{4,3,2,1,0:T(8,128)(2,1)S(1)} %copy-done.2, bf16[1,2,32,1024]{3,2,1,0:T(8,128)(2,1)} %reduce-scatter.2.cloned.1.call-done), kind=kLoop, calls=%fused_computation.30 | loop fusion | flops 458752 | bytes 655360 | tf_op jit(solution)/shard_map/convert_element_type | solution.py:75
  (7 shorter events, 0.2 us)
Async XLA Ops:
  6.5 5.7 %copy-start = (bf16[1,1,2,32,64,128]{5,4,3,2,1,0:T(8,128)(2,1)S(1)}, bf16[1,1,2,32,64,128]{5,4,3,2,1,0:T(8,128)(2,1)}, u32[]{:S(2)}) copy-start(bf16[1,1,2,32,64,128]{5,4,3,2,1,0:T(8,128)(2,1)} %param.13) | copy-start | bytes 3145732
  6.5 31.9 %all-gather.2.cloned.1.call-start = ((), (), s32[]{:S(2)}) async-start(), calls=%async_computation.1 | async-start | bytes 1179648 | tf_op jit(solution)/shard_map/all_gather | solution.py:43
  10.0 2.8 %copy-start.2 = (bf16[1,1,2,32,1024]{4,3,2,1,0:T(8,128)(2,1)S(1)}, bf16[1,1,2,32,1024]{4,3,2,1,0:T(8,128)(2,1)}, u32[]{:S(2)}) copy-start(bf16[1,1,2,32,1024]{4,3,2,1,0:T(8,128)(2,1)} %param.17) | copy-start | bytes 393220
  12.0 1.6 %copy-start.4 = (bf16[4096]{0:T(1024)(128)(2,1)S(1)}, bf16[4096]{0:T(1024)(128)(2,1)}, u32[]{:S(2)}) copy-start(bf16[4096]{0:T(1024)(128)(2,1)} %param.18) | copy-start | bytes 24580
  13.5 99.6 %reduce-scatter.2.cloned.1.call-start = ((), (), s32[]{:S(2)}) async-start(), calls=%async_computation.2 | async-start | bytes 1179648 | tf_op jit(solution)/shard_map/reduce_scatter | solution.py:69
  40.0 8.7 %copy-start.3 = (f32[2,2,32]{2,1,0:T(2,128)}, f32[2,2,32]{2,1,0:T(2,128)S(1)}, u32[]{:S(2)}) copy-start(f32[2,2,32]{2,1,0:T(2,128)S(1)} %add_rsqrt_fusion) | copy-start | bytes 1540
  40.0 8.7 %copy-start.1 = (bf16[8,2,32,1024]{3,2,1,0:T(8,128)(2,1)S(1)}, bf16[8,2,32,1024]{3,2,1,0:T(8,128)(2,1)}, u32[]{:S(2)}) copy-start(bf16[8,2,32,1024]{3,2,1,0:T(8,128)(2,1)} %all-gather.2.cloned.1.call-done) | copy-start | bytes 3145732
Sparse Core Ops, SparseCore 0:
  13.6 24.7 all-gather.1
  75.0 38.0 reduce-scatter.1
where the time goes:
time: 122 us
  waiting for transfers between devices  38.5 us (32%)
  matrix products  37.1 us (30%)
  local copies, waits for them, and re-layouts  26.7 us (22%)
  between operations  13.5 us (11%)
  other arithmetic  5.66 us (5%)
    reduce_scatter x1, waiting for transfers between devices, feed_forward(): lax.psum_scatter(partial_term.reshape(groups * devices, batches, rows, wi...  38.2 us
    dot_general x1, matrix products, feed_forward(): jnp.einsum('abmrf,fkc->abkmrc', hidden, w_down.reshape(local_units, KV_HE...  25.1 us
    reshape x1, local copies, waits for them, and re-layouts, feed_forward(): w_down.reshape(local_units, KV_HEADS, width)  24.5 us
    dot_general x1, matrix products, feed_forward(): jnp.einsum('abkmrc,kcf->abmrf', normed, w_gate.reshape(KV_HEADS, width, l...  8.64 us
  transfers between devices with their start and end apart: 2, of which 2 were waited for; matrix products, arithmetic and copies ran while one was open for 20% of the time, Pallas kernels for 0%

commit v1 on v0

v1 whole, which is shorter than its diff:
```python
import functools

import jax
import jax.numpy as jnp
from jax import lax
from jax.experimental import pallas as pl
from jax.experimental.pallas import tpu as pltpu
from jax.sharding import PartitionSpec as P

KV_HEADS = 4
MIB = 1 << 20
LONG = 20000000000
LOG2E = 1.4426950408889634
PREP = 3000000000
COSTS = (LONG, 2000000000)
VMEM = pl.BlockSpec(memory_space=pltpu.VMEM)
HBM = pl.BlockSpec(memory_space=pltpu.HBM)


def params(limit=2 * MIB):
    return pltpu.CompilerParams(vmem_limit_bytes=limit)


def in_hbm(x):
    return pltpu.with_memory_space_constraint(x, pltpu.HBM)


def cost(flops, bytes_accessed):
    return pl.CostEstimate(flops=flops, bytes_accessed=bytes_accessed, transcendentals=0)


def peer(offset):
    return lax.axis_index("dev") ^ offset


def head_start(offset, width):
    return pl.multiple_of(lax.rem(peer(offset), KV_HEADS) * width, width)


def block_start(devices, offset, rows):
    if devices == KV_HEADS:
        return 0
    return pl.multiple_of(peer(offset) // KV_HEADS * rows, rows)


def column_tiles(units, tile=256):
    return [slice(c, min(c + tile, units)) for c in range(0, units, tile)]


def attend_rows(len_of, relative, q_ref, k_ref, v_ref, kn_ref, vn_ref, res_ref):
    part, width = q_ref.shape
    head = kn_ref.shape[-1]
    heads = width // head
    groups = part // 8
    span = k_ref.shape[0] // groups
    factor = head ** (-0.5) * LOG2E
    sub = lax.broadcasted_iota(jnp.int32, (8, 128), 0)
    wide = q_ref[...].astype(jnp.float32)
    fresh_keys = kn_ref[...].astype(jnp.float32)
    fresh_values = vn_ref[...].astype(jnp.float32)
    spread, keys_spread, biases = [], [], []
    for g in range(groups):
        own = slice(8 * g, 8 * g + 8)
        spread += [wide[own, i * head : (i + 1) * head] for i in range(heads)]
        keys_spread += [fresh_keys[own]] * heads
        limit = jnp.zeros((8, 128), jnp.int32)
        for r in range(8):
            limit = jnp.where(sub == r, len_of(8 * g + r), limit)
        limit = jnp.concatenate([limit] * (span // 128), axis=1)
        bias = jnp.where(relative < limit, 0.0, -1e30)
        biases.append(jnp.concatenate([bias] * heads, axis=0))
    q = jnp.concatenate(spread, axis=0)
    fresh = jnp.sum(q * jnp.concatenate(keys_spread, axis=0), axis=-1, keepdims=True)
    q = q.astype(jnp.bfloat16)
    scores = []
    for g in range(groups):
        scores.append(
            lax.dot_general(
                q[8 * heads * g : 8 * heads * (g + 1)],
                k_ref[g * span : (g + 1) * span, :],
                (((1,), (1,)), ((), ())),
                preferred_element_type=jnp.float32,
            )
            + biases[g]
        )
    scores = jnp.concatenate(scores, axis=0)
    top = jnp.maximum(jnp.max(scores, axis=-1, keepdims=True), fresh)
    weights = jnp.exp2((scores - top) * factor)
    own_weight = jnp.exp2((fresh - top) * factor)
    inverse = 1.0 / (jnp.sum(weights, axis=-1, keepdims=True) + own_weight)
    own_weight = own_weight * inverse
    weights = weights.astype(jnp.bfloat16)
    rows = []
    for g in range(groups):
        mine = slice(8 * heads * g, 8 * heads * (g + 1))
        attended = jnp.dot(weights[mine], v_ref[g * span : (g + 1) * span, :], preferred_element_type=jnp.float32)
        own = jnp.concatenate([fresh_values[8 * g : 8 * g + 8]] * heads, axis=0)
        attended = attended * inverse[mine] + own_weight[mine] * own
        rows.append(jnp.concatenate([attended[8 * i : 8 * i + 8] for i in range(heads)], axis=1))
    return (res_ref[...].astype(jnp.float32) + jnp.concatenate(rows, axis=0)).astype(jnp.bfloat16)


def relative_positions(cache):
    lane = lax.broadcasted_iota(jnp.int32, (8, 8 * cache), 1)
    relative = lane - cache * lax.broadcasted_iota(jnp.int32, (8, 8 * cache), 0)
    return jnp.where(relative < 0, cache, relative)


def attend_kernel(devices, batch, len_in, *refs):
    count = 6
    sources, out_ref, refs = refs[:count], refs[count], refs[count + 1 :]
    if batch == 0:
        later, refs = refs[:count], refs[count:]
        sources_later = sources
        held, refs = refs[:count], refs[count:]
    else:
        held, later = sources, ()
    len_ref, sem = refs
    block = lax.axis_index("dev") // KV_HEADS if devices > KV_HEADS else 0
    lengths = pltpu.make_async_copy(len_in, len_ref, sem.at[2 * count])
    lengths.start()
    copies = []
    if batch == 0:
        for n in (0, 3, 1, 2, 4, 5):
            rows = held[n].shape[0]
            copies.append(pltpu.make_async_copy(sources[n].at[pl.ds(0, rows)], held[n], sem.at[n]))
        for n in (1, 2, 0, 3, 4, 5):
            rows = held[n].shape[0]
            copies.append(pltpu.make_async_copy(sources_later[n].at[pl.ds(rows, rows)], later[n], sem.at[count + n]))
        for copy in copies:
            copy.start()
    cache = held[1].shape[0] // held[0].shape[0]
    relative = relative_positions(cache)
    lengths.wait()
    for copy in copies[:count]:
        copy.wait()
    out_ref[...] = attend_rows(lambda r: len_ref[block, batch, r], relative, *held)
    for copy in copies[count:]:
        copy.wait()


def attend(devices, batch, lengths, *arrays):
    rows = arrays[0].shape[0] // (2 if batch == 0 else 1)
    width = arrays[0].shape[1]
    shapes = [pltpu.VMEM((rows, width), jnp.bfloat16)]
    scratch = []
    if batch == 0:
        halves = [(a.shape[0] // 2,) + a.shape[1:] for a in arrays]
        shapes += [pltpu.VMEM(shape, a.dtype) for shape, a in zip(halves, arrays)]
        scratch = [pltpu.VMEM(shape, a.dtype) for shape, a in zip(halves, arrays)]
    return pl.pallas_call(
        functools.partial(attend_kernel, devices, batch),
        out_shape=shapes,
        in_specs=[HBM] + [HBM if batch == 0 else VMEM] * len(arrays),
        out_specs=[VMEM] * len(shapes),
        scratch_shapes=scratch
        + [pltpu.SMEM(lengths.shape, lengths.dtype), pltpu.SemaphoreType.DMA((2 * len(arrays) + 1,))],
        compiler_params=params(4 * MIB),
        cost_estimate=cost(COSTS[batch], 0),
        name="attend",
    )(lengths, *arrays)


def silu_product(gate, up):
    return (gate / (1.0 + jnp.exp(-gate)) * up).astype(jnp.bfloat16)


def place_rows(devices, offsets, pieces, x_ref):
    rows, width = pieces[0].shape
    for n, offset in enumerate(offsets):
        lanes = pl.ds(head_start(offset, width), width)
        part = pl.ds(block_start(devices, offset, rows), rows)
        for side in range(2):
            x_ref[side, part, lanes] = pieces[2 * n + side][...]


def normalize(x_ref, gain_ref, out_ref):
    gain = gain_ref[...].astype(jnp.float32).reshape(1, gain_ref.shape[0])
    for side in range(2):
        for part in range(x_ref.shape[1] // 16):
            stripe = slice(16 * part, 16 * part + 16)
            x = x_ref[side, stripe, :].astype(jnp.float32)
            inverse = lax.rsqrt(jnp.mean(x * x, axis=-1, keepdims=True) + 1e-05)
            out_ref[side, stripe, :] = (x * inverse * gain).astype(jnp.bfloat16)


def prepare_kernel(devices, offsets, gain_ref, *refs):
    pieces, (out_ref, x_ref) = refs[:-2], refs[-2:]
    place_rows(devices, offsets, pieces, x_ref)
    normalize(x_ref, gain_ref, out_ref)


def prepare(devices, offsets, pieces, gain):
    rows, width = pieces[0].shape
    blocks = devices // KV_HEADS
    shape = (2, blocks * rows, KV_HEADS * width)
    return pl.pallas_call(
        functools.partial(prepare_kernel, devices, offsets),
        out_shape=pltpu.VMEM(shape, jnp.bfloat16),
        in_specs=[VMEM] * (1 + len(pieces)),
        out_specs=VMEM,
        scratch_shapes=[pltpu.VMEM(shape, jnp.bfloat16)],
        compiler_params=params(blocks * 2 * MIB),
        cost_estimate=cost(PREP, 0),
        name="prepare",
    )(gain, *pieces)


def hidden_kernel(devices, offsets, gain_ref, wg_ref, wu_ref, wd_ref, ready_ref, *refs):
    del wd_ref
    pieces, (hidden_ref, late_ref, x_ref) = refs[:-3], refs[-3:]
    rows, _ = pieces[0].shape
    total, units = hidden_ref.shape
    place_rows(devices, offsets, pieces, late_ref)
    normalize(late_ref, gain_ref, late_ref)
    for block in range(devices // KV_HEADS):
        part = slice(block * rows, (block + 1) * rows)
        for side in range(2):
            for batch, ref in enumerate((ready_ref, late_ref)):
                row = (4 * block + 2 * side + batch) * rows
                x_ref[row : row + rows, :] = ref[side, part, :]
    x = x_ref[...]
    for lanes in column_tiles(units):
        gate = jnp.dot(x, wg_ref[:, lanes], preferred_element_type=jnp.float32)
        up = jnp.dot(x, wu_ref[:, lanes], preferred_element_type=jnp.float32)
        hidden_ref[:, lanes] = silu_product(gate, up)


def hidden_units(devices, offsets, ready, pieces, gain, w_gate, w_up, w_down):
    features, units = w_gate.shape
    total = 2 * ready.shape[0] * ready.shape[1]
    return pl.pallas_call(
        functools.partial(hidden_kernel, devices, offsets),
        out_shape=pltpu.VMEM((total, units), jnp.bfloat16),
        in_specs=[VMEM] * (5 + len(pieces)),
        out_specs=VMEM,
        scratch_shapes=[pltpu.VMEM(ready.shape, jnp.bfloat16), pltpu.VMEM((total, features), jnp.bfloat16)],
        compiler_params=params(devices // KV_HEADS * 5 * MIB),
        cost_estimate=cost(4 * total * features * units, 0),
        name="hidden",
    )(gain, w_gate, w_up, w_down, ready, *pieces)


def down_kernel(devices, offsets, hidden_ref, weight_ref, *refs):
    keep_ref, send_ref = refs[-2:]
    _, rows, width = keep_ref.shape
    for n, offset in enumerate(offsets):
        mine = pl.ds(block_start(devices, offset, 2 * rows), 2 * rows)
        hidden = hidden_ref[mine, :]
        for lanes in column_tiles(width):
            size = lanes.stop - lanes.start
            column = pl.multiple_of(head_start(offset, width) + lanes.start, size)
            term = jnp.dot(hidden, weight_ref[:, pl.ds(column, size)], preferred_element_type=jnp.float32)
            keep_ref[n, :, lanes] = term[:rows]
            send_ref[n, :, lanes] = term[rows:].astype(jnp.bfloat16)


def down(devices, offsets, hidden, w_down, rows, after=()):
    units, features = w_down.shape
    width = features // KV_HEADS
    shape = (len(offsets), rows, width)
    return pl.pallas_call(
        functools.partial(down_kernel, devices, offsets),
        out_shape=[pltpu.VMEM(shape, jnp.float32), pltpu.VMEM(shape, jnp.bfloat16)],
        in_specs=[VMEM] * 2 + [pl.BlockSpec(memory_space=pl.ANY)] * len(after),
        out_specs=[VMEM] * 2,
        compiler_params=params(),
        cost_estimate=cost(4 * rows * width * units * len(offsets), 0),
        name="down",
    )(hidden, w_down, *after)


def fold_kernel(offsets, count, *refs):
    keep_ref, got_ref = refs[:2]
    more, out_refs = refs[2 : 2 + count], refs[-len(offsets) :]
    for n, out_ref in enumerate(out_refs):
        term = keep_ref[n] + got_ref[n].astype(jnp.float32)
        for ref in more:
            term = term + ref[...].astype(jnp.float32)
        out_ref[...] = term.astype(out_ref.dtype)


def fold(offsets, keep, got, more=(), after=(), flops=0):
    _, rows, width = keep.shape
    return pl.pallas_call(
        functools.partial(fold_kernel, offsets, len(more)),
        out_shape=[pltpu.VMEM((rows, width), jnp.float32 if o == 0 else jnp.bfloat16) for o in offsets],
        in_specs=[VMEM] * (2 + len(more)) + [pl.BlockSpec(memory_space=pl.ANY)] * len(after),
        out_specs=[VMEM] * len(offsets),
        compiler_params=params(),
        cost_estimate=cost(flops, 0),
        name="fold",
    )(keep, got, *more, *after)


def finish_kernel(first_ref, second_ref, *refs):
    out_ref = refs[-1]
    rows = first_ref.shape[0]
    for n, stream_ref in enumerate((first_ref, second_ref)):
        part = slice(n * rows, (n + 1) * rows)
        total = stream_ref[...].astype(jnp.float32)
        for ref in refs[:-1]:
            total = total + ref[part, :].astype(jnp.float32)
        out_ref[part, :] = total.astype(out_ref.dtype)


def finish(streams, terms):
    return pl.pallas_call(
        finish_kernel,
        out_shape=jax.ShapeDtypeStruct(terms[0].shape, jnp.bfloat16),
        compiler_params=params(),
        name="finish",
    )(*streams, *terms)


def swap(x):
    return lax.ppermute(x, "att", [(0, 1), (1, 0)])


def exchange(x, offset, devices):
    return lax.ppermute(x, "dev", [(i, i ^ offset) for i in range(devices)])


def shards(
    query, key_cache, value_cache, key_new, value_new, lengths, resid, gain, w_gate, w_up, w_down
):
    devices = lax.axis_size("dev")
    width = query.shape[-1]
    head = key_cache.shape[-1]
    lengths = in_hbm(lengths[0])
    first, *rest = attend(
        devices,
        0,
        lengths,
        in_hbm(query.reshape(-1, width)),
        in_hbm(key_cache.reshape(-1, head)),
        in_hbm(value_cache.reshape(-1, head)),
        in_hbm(key_new.reshape(-1, head)),
        in_hbm(value_new.reshape(-1, head)),
        in_hbm(resid.reshape(-1, width)),
    )
    (second,) = attend(devices, 1, lengths, *rest)
    streams = (first, second)
    rows = 2 * first.shape[0]
    offsets = tuple(range(devices))
    arrived = []
    for stream in streams:
        pieces = {0: stream}
        bit = devices // 2
        while bit:
            for o in tuple(pieces):
                pieces[o ^ bit] = exchange(pieces[o], bit, devices)
            bit //= 2
        arrived.append([x for o in offsets for x in (pieces[o], swap(pieces[o]))])
    ready = prepare(devices, offsets, arrived[0], gain)
    hidden = hidden_units(devices, offsets, ready, arrived[1], gain, w_gate, w_up, w_down)

    def part(offsets, after=()):
        keep, send = down(devices, offsets, hidden, w_down, rows, after)
        return offsets, keep, swap(send)

    if devices == 4:
        (third,) = fold(*part((3,)))
        relayed = exchange(third, 1, devices)
        second_parts = part((2,))
        nearer_parts = part((1, 0), (third,))
        (second,) = fold(*second_parts, (relayed,), (), LONG)
        first, own = fold(*nearer_parts, (), (second,))
        terms = [own, exchange(first, 1, devices), exchange(second, 2, devices)]
    else:
        terms = {}
        for start in range(devices - 2, -1, -2):
            offsets = (start + 1, start)
            for o, term in zip(offsets, fold(*part(offsets))):
                terms[o] = term if o == 0 else exchange(term, o, devices)
        terms = [terms[o] for o in range(devices)]
    return finish(streams, terms).reshape(query.shape)


def solution(mesh):
    return jax.shard_map(
        shards,
        mesh=mesh,
        in_specs=(
            P(("grp", "att"), "dev", None, None, None),
            P(("grp", "att"), "dev", None, None, None, None),
            P(("grp", "att"), "dev", None, None, None, None),
            P(("grp", "att"), "dev", None, None, None),
            P(("grp", "att"), "dev", None, None, None),
            P(("grp", "att"), None, None, None),
            P(("grp", "att"), "dev", None, None, None),
            P(),
            P(None, ("att", "dev")),
            P(None, ("att", "dev")),
            P(("att", "dev"), None),
        ),
        out_specs=P(("grp", "att"), "dev", None, None, None),
        check_vma=False,
    )
```

time: 122 us -> 41.9 us (0.34)
  matrix products: 37.1 us -> 0 us
  waiting for transfers between devices: 38.5 us -> 10.5 us
  local copies, waits for them, and re-layouts: 26.7 us -> 0.06 us
  starting transfers between devices: 0.04 us -> 18.8 us
  between operations: 13.5 us -> 0.28 us
  Pallas kernels: 0 us -> 12 us
  other arithmetic: 5.66 us -> 0.01 us
    reduce_scatter x1 -> x0, waiting for transfers between devices: 38.2 us -> none  [feed_forward(): lax.psum_scatter(partial_term.reshape(groups * devices, batches, rows, wi...]
    dot_general x5 -> x0, matrix products: 37.1 us -> none  [the longest x1 25.1 us: feed_forward(): jnp.einsum('abmrf,fkc->abkmrc', hidden, w_down.reshape(local_units, KV_HE...]
    reshape x3 -> x0, local copies, waits for them, and re-layouts: 24.6 us -> none  [the longest x1 24.5 us: feed_forward(): w_down.reshape(local_units, KV_HEADS, width)]
    ppermute x0 -> x20, starting transfers between devices: none -> 18.8 us  [the longest x9 16.5 us: exchange(): return lax.ppermute(x, 'dev', [(i, i ^ offset) for i in range(devices)])]
    pallas_call x0 -> x11, Pallas kernels: none -> 12 us  [the longest x1 4.59 us: hidden_units(): pl.pallas_call(functools.partial(hidden_kernel, devices, offsets), out_sh...]
    ppermute x0 -> x20, waiting for transfers between devices: none -> 10.5 us  [the longest x9 9.56 us: exchange(): return lax.ppermute(x, 'dev', [(i, i ^ offset) for i in range(devices)])]
    convert_element_type x3 -> x0, other arithmetic: 3.01 us -> none  [the longest x1 1.6 us: feed_forward(): return (stream_rows.astype(jnp.float32) + combined).astype(jnp.bfloat16)]
    reduce_sum x3 -> x0, other arithmetic: 1.77 us -> none  [the longest x2 1.52 us: feed_forward(): mean_square = jnp.mean(widened * widened, axis=(2, 5), keepdims=True)]
  transfers between devices with their start and end apart: 2 -> 20, of which waited for: 2 -> 10; matrix products, arithmetic and copies ran while one was open for 20% -> 0% of each run, Pallas kernels for 0% -> 9%
where the time goes in v1:
time: 41.9 us; the launch traced here: 41.7 us
  starting transfers between devices  18.8 us (45%)
  Pallas kernels  12 us (29%)
  waiting for transfers between devices  10.5 us (25%)
    ppermute x9, starting transfers between devices, exchange(): return lax.ppermute(x, 'dev', [(i, i ^ offset) for i in range(devices)])  16.5 us
    ppermute x9, waiting for transfers between devices, exchange(): return lax.ppermute(x, 'dev', [(i, i ^ offset) for i in range(devices)])  9.56 us
    pallas_call x1, Pallas kernels, hidden_units(): pl.pallas_call(functools.partial(hidden_kernel, devices, offsets), out_sh...  4.59 us
    pallas_call x2, Pallas kernels, attend(): pl.pallas_call(functools.partial(attend_kernel, devices, batch), out_shap...  3.56 us
    pallas_call x3, Pallas kernels, down(): pl.pallas_call(functools.partial(down_kernel, devices, offsets), out_shap...  2.73 us
    ppermute x11, starting transfers between devices, swap(): return lax.ppermute(x, 'att', [(0, 1), (1, 0)])  2.3 us
    ppermute x11, waiting for transfers between devices, swap(): return lax.ppermute(x, 'att', [(0, 1), (1, 0)])  0.92 us
  transfers between devices with their start and end apart: 20, of which 10 were waited for; matrix products, arithmetic and copies ran while one was open for 0% of the time, Pallas kernels for 9%

profile of v1, /device:TPU:0, one launch (start us, length us, event | category | flops | bytes accessed | tf_op | source)
XLA Modules:
  0.0 41.7 jit_solution(4367702910217844836)
XLA Ops:
  0.1 2.1 %attend.2 = (bf16[32,1024]{1,0:T(8,128)(2,1)S(1)}, bf16[32,1024]{1,0:T(8,128)(2,1)S(1)}, bf16[2048,128]{1,0:T(8,128)(2,1)S(1)}, bf16[2048,128]{1,0:T(8,128)(2,1)...) custom-call(s32[1,2,32]{2,1,0:T(2,128)} %bitcast.20, ...), custom_call_target="tpu_custom_call" | custom-call | flops 20000000000 | tf_op jit(solution)/shard_map/attend/pallas_call | solution.py:151
  2.2 4.1 %collective-permute-start.3 = (bf16[32,1024]{1,0:T(8,128)(2,1)S(1)}, bf16[32,1024]{1,0:T(8,128)(2,1)S(1)}, u32[]{:S(2)}, u32[]{:S(2)}) collective-permute-start(bf16[32,1024]{1,0:T(8,128)(2,1)S(1)} %get-tuple-element.20.refs_0_.first_ref), channel_id=1, source_target_pairs={{0,2},{1,3},{2,0},{3,1},{4,6},{5,7},{6,4},{7,5},{8,10},{9,11},{10,... | collective-permute-start | bytes 196616 | tf_op jit(solution)/shard_map/ppermute | solution.py:321
  6.3 1.5 %attend.3.refs_0_.second_ref = bf16[32,1024]{1,0:T(8,128)(2,1)S(1)} custom-call(s32[1,2,32]{2,1,0:T(2,128)} %bitcast.21, bf16[32,1024]{1,0:T(8,128)(2,1)S(1)} %get-tuple-element.21.refs_0_, bf16[2048,128]{1,0:T(8,128)(2,1)S(1)} %get-tuple-element.22.refs_1_, bf16[2048,128]{1,0:T(8,128)(2,1)S(1)} %get-tuple-element.23.refs_2_, ...), custom_call_target="tpu_custom_call" | custom-call | flops 2000000000 | tf_op jit(solution)/shard_map/attend/pallas_call | solution.py:151
  7.8 0.1 collective-permute-start.10
  7.9 1.9 %collective-permute-start.8 = (bf16[32,1024]{1,0:T(8,128)(2,1)S(1)}, bf16[32,1024]{1,0:T(8,128)(2,1)S(1)}, u32[]{:S(2)}, u32[]{:S(2)}) collective-permute-start(bf16[32,1024]{1,0:T(8,128)(2,1)S(1)} %attend.3.refs_0_.second_ref), channel_id=1, source_target_pairs={{0,1},{1,0},{2,3},{3,2},{4,5},{5,4},{6,7},{7,6},{8,9},{9,8},{10,11... | collective-permute-start | bytes 196616 | tf_op jit(solution)/shard_map/ppermute | solution.py:321
  9.8 0.2 collective-permute-start.1
  10.0 2.3 %collective-permute-start.5 = (bf16[32,1024]{1,0:T(8,128)(2,1)S(1)}, bf16[32,1024]{1,0:T(8,128)(2,1)S(1)}, u32[]{:S(2)}, u32[]{:S(2)}) collective-permute-start(bf16[32,1024]{1,0:T(8,128)(2,1)S(1)} %collective-permute-done.3.refs_4_), channel_id=1, source_target_pairs={{0,1},{1,0},{2,3},{3,2},{4,5},{5,4},{6,7},{7,6},{8,9},{9,8},{10,11... | collective-permute-start | bytes 196616 | tf_op jit(solution)/shard_map/ppermute | solution.py:321
  12.2 1.2 %collective-permute-done.10.refs_4_ = bf16[32,1024]{1,0:T(8,128)(2,1)S(1)} collective-permute-done((bf16[32,1024]{1,0:T(8,128)(2,1)S(1)}, bf16[32,1024]{1,0:T(8,128)(2,1)S(1)}, u32[]{:S(2)}, u32[]{:S(2)}) %collective-permute-start.10) | collective-permute-done | bytes 65568 | tf_op jit(solution)/shard_map/ppermute | solution.py:321
  13.4 1.8 %collective-permute-start.12 = (bf16[32,1024]{1,0:T(8,128)(2,1)S(1)}, bf16[32,1024]{1,0:T(8,128)(2,1)S(1)}, u32[]{:S(2)}, u32[]{:S(2)}) collective-permute-start(bf16[32,1024]{1,0:T(8,128)(2,1)S(1)} %collective-permute-done.10.refs_4_), channel_id=1, source_target_pairs={{0,1},{1,0},{2,3},{3,2},{4,5},{5,4},{6,7},{7,6},{8,9},{9,8},{10,11... | collective-permute-start | bytes 196616 | tf_op jit(solution)/shard_map/ppermute | solution.py:321
  15.3 0.5 %collective-permute-start.2 = (bf16[32,1024]{1,0:T(8,128)(2,1)S(1)}, bf16[32,1024]{1,0:T(8,128)(2,1)S(1)}, u32[]{:S(2)}, u32[]{:S(2)}) collective-permute-start(bf16[32,1024]{1,0:T(8,128)(2,1)S(1)} %collective-permute-done.1.refs_2_), channel_id=1, source_target_pairs={{0,4},{4,0},{1,5},{5,1},{2,6},{6,2},{3,7},{7,3},{8,12},{12,8},{9,1... | collective-permute-start | bytes 196616 | tf_op jit(solution)/shard_map/ppermute | solution.py:317
  15.8 0.5 %collective-permute-done.5.refs_6_ = bf16[32,1024]{1,0:T(8,128)(2,1)S(1)} collective-permute-done((bf16[32,1024]{1,0:T(8,128)(2,1)S(1)}, bf16[32,1024]{1,0:T(8,128)(2,1)S(1)}, u32[]{:S(2)}, u32[]{:S(2)}) %collective-permute-start.5) | collective-permute-done | bytes 65568 | tf_op jit(solution)/shard_map/ppermute | solution.py:321
  16.2 0.5 %collective-permute-start.7 = (bf16[32,1024]{1,0:T(8,128)(2,1)S(1)}, bf16[32,1024]{1,0:T(8,128)(2,1)S(1)}, u32[]{:S(2)}, u32[]{:S(2)}) collective-permute-start(bf16[32,1024]{1,0:T(8,128)(2,1)S(1)} %attend.3.refs_0_.second_ref), channel_id=1, source_target_pairs={{0,4},{4,0},{1,5},{5,1},{2,6},{6,2},{3,7},{7,3},{8,12},{12,8},{9,1... | collective-permute-start | bytes 196616 | tf_op jit(solution)/shard_map/ppermute | solution.py:317
  16.8 0.9 %collective-permute-done.12.refs_6_ = bf16[32,1024]{1,0:T(8,128)(2,1)S(1)} collective-permute-done((bf16[32,1024]{1,0:T(8,128)(2,1)S(1)}, bf16[32,1024]{1,0:T(8,128)(2,1)S(1)}, u32[]{:S(2)}, u32[]{:S(2)}) %collective-permute-start.12) | collective-permute-done | bytes 65568 | tf_op jit(solution)/shard_map/ppermute | solution.py:321
  17.7 0.5 %collective-permute-start.9 = (bf16[32,1024]{1,0:T(8,128)(2,1)S(1)}, bf16[32,1024]{1,0:T(8,128)(2,1)S(1)}, u32[]{:S(2)}, u32[]{:S(2)}) collective-permute-start(bf16[32,1024]{1,0:T(8,128)(2,1)S(1)} %collective-permute-done.8.refs_2_), channel_id=1, source_target_pairs={{0,4},{4,0},{1,5},{5,1},{2,6},{6,2},{3,7},{7,3},{8,12},{12,8},{9,1... | collective-permute-start | bytes 196616 | tf_op jit(solution)/shard_map/ppermute | solution.py:317
  18.3 0.3 prepare.1.ready_ref
  18.6 0.3 collective-permute-done.11.refs_5_
  18.9 0.2 collective-permute-done.9.refs_3_
  19.1 0.4 collective-permute-done.13.refs_7_
  19.6 4.6 %hidden.1.hidden_ref = bf16[128,1792]{1,0:T(8,128)(2,1)S(1)} custom-call(bf16[4096]{0:T(1024)(128)(2,1)S(1)} %copy-done, bf16[4096,1792]{1,0:T(8,128)(2,1)S(1)} %bitcast.11, bf16[4096,1792]{1,0:T(8,128)(2,1)S(1)} %bitcast.13, bf16[1792,4096]{1,0:T(8,128)(2,1)S(1)} %bitcast.9, bf16[2,32,4096]{2,1,0:T(8,128)(2,1)S(1)} %prepare.1.ready_ref, ...), custom_call_target="tpu_custom_call" | custom-call | flops 3758096384 | tf_op jit(solution)/shard_map/hidden/pallas_call | solution.py:232
  24.2 0.7 %down.3 = (f32[1,64,1024]{2,1,0:T(8,128)S(1)}, bf16[1,64,1024]{2,1,0:T(8,128)(2,1)S(1)}) custom-call(bf16[128,1792]{1,0:T(8,128)(2,1)S(1)} %hidden.1.hidden_ref, bf16[1792,4096]{1,0:T(8,128)(2,1)S(1)} %bitcast.9), custom_call_target="tpu_custom_call" | custom-call | flops 469762048 | tf_op jit(solution)/shard_map/down/pallas_call | solution.py:262
  24.9 0.2 collective-permute-start.14
  25.1 0.7 %down.5 = (f32[1,64,1024]{2,1,0:T(8,128)S(1)}, bf16[1,64,1024]{2,1,0:T(8,128)(2,1)S(1)}) custom-call(bf16[128,1792]{1,0:T(8,128)(2,1)S(1)} %hidden.1.hidden_ref, bf16[1792,4096]{1,0:T(8,128)(2,1)S(1)} %bitcast.9), custom_call_target="tpu_custom_call" | custom-call | flops 469762048 | tf_op jit(solution)/shard_map/down/pallas_call | solution.py:262
  25.9 0.4 %collective-permute-start.16 = (bf16[1,64,1024]{2,1,0:T(8,128)(2,1)S(1)}, bf16[1,64,1024]{2,1,0:T(8,128)(2,1)S(1)}, u32[]{:S(2)}, u32[]{:S(2)}) collective-permute-start(bf16[1,64,1024]{2,1,0:T(8,128)(2,1)S(1)} %get-tuple-element.32), channel_id=1, source_target_pairs={{0,4},{4,0},{1,5},{5,1},{2,6},{6,2},{3,7},{7,3},{8,12},{12,8},{9,1... | collective-permute-start | bytes 393224 | tf_op jit(solution)/shard_map/ppermute | solution.py:317
  26.4 1.9 %collective-permute-start.17 = (bf16[64,1024]{1,0:T(8,128)(2,1)S(1)}, bf16[64,1024]{1,0:T(8,128)(2,1)S(1)}, u32[]{:S(2)}, u32[]{:S(2)}) collective-permute-start(bf16[64,1024]{1,0:T(8,128)(2,1)S(1)} %fold.3.refs_0_), channel_id=1, source_target_pairs={{0,1},{1,0},{2,3},{3,2},{4,5},{5,4},{6,7},{7,6},{8,9},{9,8},{10,11... | collective-permute-start | bytes 393224 | tf_op jit(solution)/shard_map/ppermute | solution.py:321
  28.3 1.3 %down.4 = (f32[2,64,1024]{2,1,0:T(8,128)S(1)}, bf16[2,64,1024]{2,1,0:T(8,128)(2,1)S(1)}) custom-call(bf16[128,1792]{1,0:T(8,128)(2,1)S(1)} %hidden.1.hidden_ref, bf16[1792,4096]{1,0:T(8,128)(2,1)S(1)} %bitcast.9, bf16[64,1024]{1,0:T(8,128)(2,1)S(1)} %fold.3.refs_0_), custom_call_target="tpu_custom_call" | custom-call | flops 939524096 | tf_op jit(solution)/shard_map/down/pallas_call | solution.py:262
  29.5 0.1 collective-permute-start.15
  29.6 2.5 %collective-permute-done.17.refs_2_ = bf16[64,1024]{1,0:T(8,128)(2,1)S(1)} collective-permute-done((bf16[64,1024]{1,0:T(8,128)(2,1)S(1)}, bf16[64,1024]{1,0:T(8,128)(2,1)S(1)}, u32[]{:S(2)}, u32[]{:S(2)}) %collective-permute-start.17) | collective-permute-done | bytes 131104 | tf_op jit(solution)/shard_map/ppermute | solution.py:321
  32.1 2.7 %collective-permute-start.19 = (bf16[64,1024]{1,0:T(8,128)(2,1)S(1)}, bf16[64,1024]{1,0:T(8,128)(2,1)S(1)}, u32[]{:S(2)}, u32[]{:S(2)}) collective-permute-start(bf16[64,1024]{1,0:T(8,128)(2,1)S(1)} %fold.4.refs_2_), channel_id=1, source_target_pairs={{0,2},{1,3},{2,0},{3,1},{4,6},{5,7},{6,4},{7,5},{8,10},{9,11},{10,... | collective-permute-start | bytes 393224 | tf_op jit(solution)/shard_map/ppermute | solution.py:321
  34.8 1.7 %collective-permute-start.18 = (bf16[64,1024]{1,0:T(8,128)(2,1)S(1)}, bf16[64,1024]{1,0:T(8,128)(2,1)S(1)}, u32[]{:S(2)}, u32[]{:S(2)}) collective-permute-start(bf16[64,1024]{1,0:T(8,128)(2,1)S(1)} %get-tuple-element.34), channel_id=1, source_target_pairs={{0,1},{1,0},{2,3},{3,2},{4,5},{5,4},{6,7},{7,6},{8,9},{9,8},{10,11... | collective-permute-start | bytes 393224 | tf_op jit(solution)/shard_map/ppermute | solution.py:321
  36.5 4.2 %collective-permute-done.19.refs_2_ = bf16[64,1024]{1,0:T(8,128)(2,1)S(1)} collective-permute-done((bf16[64,1024]{1,0:T(8,128)(2,1)S(1)}, bf16[64,1024]{1,0:T(8,128)(2,1)S(1)}, u32[]{:S(2)}, u32[]{:S(2)}) %collective-permute-start.19) | collective-permute-done | bytes 131104 | tf_op jit(solution)/shard_map/ppermute | solution.py:321
  40.7 0.3 collective-permute-done.18.refs_1_
  41.0 0.7 %finish.1 = bf16[64,1024]{1,0:T(8,128)(2,1)} custom-call(bf16[32,1024]{1,0:T(8,128)(2,1)S(1)} %get-tuple-element.20.refs_0_.first_ref, bf16[32,1024]{1,0:T(8,128)(2,1)S(1)} %attend.3.refs_0_.second_ref, f32[64,1024]{1,0:T(8,128)S(1)} %get-tuple-element.33.refs_0_, bf16[64,1024]{1,0:T(8,128)(2,1)S(1)} %collective-permute-done.18.refs_1_, ...), custom_call_target="tpu_custom_call" | custom-call | tf_op jit(solution)/shard_map/finish/pallas_call | solution.py:308
  (48 shorter events, 0.4 us)
Async XLA Ops:
  0.0 19.5 %slice-start = ((s8[14680064]{0:T(1024)(128)(4,1)}), s8[4194304]{0:T(1024)(128)(4,1)S(1)}, s32[]{:S(2)}) async-start(s8[14680064]{0:T(1024)(128)(4,1)} %bitcast.8), calls=%async_computation | async-start | bytes 8388608
  0.0 19.5 %slice-start.4 = ((s8[14680064]{0:T(1024)(128)(4,1)}), s8[4194304]{0:T(1024)(128)(4,1)S(1)}, s32[]{:S(2)}) async-start(s8[14680064]{0:T(1024)(128)(4,1)} %bitcast.10), calls=%async_computation.4 | async-start | bytes 8388608
  0.0 19.5 %slice-start.8 = ((s8[14680064]{0:T(1024)(128)(4,1)}), s8[4194304]{0:T(1024)(128)(4,1)S(1)}, s32[]{:S(2)}) async-start(s8[14680064]{0:T(1024)(128)(4,1)} %bitcast.12), calls=%async_computation.8 | async-start | bytes 8388608
  0.0 19.5 %slice-start.1 = ((s8[14680064]{0:T(1024)(128)(4,1)}), s8[4194304]{0:T(1024)(128)(4,1)S(1)}, s32[]{:S(2)}) async-start(s8[14680064]{0:T(1024)(128)(4,1)} %bitcast.8), calls=%async_computation.1 | async-start | bytes 8388608
  0.0 19.5 %slice-start.2 = ((s8[14680064]{0:T(1024)(128)(4,1)}), s8[4194304]{0:T(1024)(128)(4,1)S(1)}, s32[]{:S(2)}) async-start(s8[14680064]{0:T(1024)(128)(4,1)} %bitcast.8), calls=%async_computation.2 | async-start | bytes 8388608
  0.0 19.5 %slice-start.3 = ((s8[14680064]{0:T(1024)(128)(4,1)}), s8[2097152]{0:T(1024)(128)(4,1)S(1)}, s32[]{:S(2)}) async-start(s8[14680064]{0:T(1024)(128)(4,1)} %bitcast.8), calls=%async_computation.3 | async-start | bytes 4194304
  0.0 19.5 %slice-start.5 = ((s8[14680064]{0:T(1024)(128)(4,1)}), s8[4194304]{0:T(1024)(128)(4,1)S(1)}, s32[]{:S(2)}) async-start(s8[14680064]{0:T(1024)(128)(4,1)} %bitcast.10), calls=%async_computation.5 | async-start | bytes 8388608
  0.0 19.5 %slice-start.6 = ((s8[14680064]{0:T(1024)(128)(4,1)}), s8[4194304]{0:T(1024)(128)(4,1)S(1)}, s32[]{:S(2)}) async-start(s8[14680064]{0:T(1024)(128)(4,1)} %bitcast.10), calls=%async_computation.6 | async-start | bytes 8388608
  0.1 19.5 %slice-start.7 = ((s8[14680064]{0:T(1024)(128)(4,1)}), s8[2097152]{0:T(1024)(128)(4,1)S(1)}, s32[]{:S(2)}) async-start(s8[14680064]{0:T(1024)(128)(4,1)} %bitcast.10), calls=%async_computation.7 | async-start | bytes 4194304
  0.1 19.5 %slice-start.9 = ((s8[14680064]{0:T(1024)(128)(4,1)}), s8[4194304]{0:T(1024)(128)(4,1)S(1)}, s32[]{:S(2)}) async-start(s8[14680064]{0:T(1024)(128)(4,1)} %bitcast.12), calls=%async_computation.9 | async-start | bytes 8388608
  0.1 19.5 %slice-start.10 = ((s8[14680064]{0:T(1024)(128)(4,1)}), s8[4194304]{0:T(1024)(128)(4,1)S(1)}, s32[]{:S(2)}) async-start(s8[14680064]{0:T(1024)(128)(4,1)} %bitcast.12), calls=%async_computation.10 | async-start | bytes 8388608
  0.1 19.5 %slice-start.11 = ((s8[14680064]{0:T(1024)(128)(4,1)}), s8[2097152]{0:T(1024)(128)(4,1)S(1)}, s32[]{:S(2)}) async-start(s8[14680064]{0:T(1024)(128)(4,1)} %bitcast.12), calls=%async_computation.11 | async-start | bytes 4194304
  2.2 7.8 %collective-permute-start.3 = (bf16[32,1024]{1,0:T(8,128)(2,1)S(1)}, bf16[32,1024]{1,0:T(8,128)(2,1)S(1)}, u32[]{:S(2)}, u32[]{:S(2)}) collective-permute-start(bf16[32,1024]{1,0:T(8,128)(2,1)S(1)} %get-tuple-element.20.refs_0_.first_ref), channel_id=1, source_target_pairs={{0,2},{1,3},{2,0},{3,1},{4,6},{5,7},{6,4},{7,5},{8,10},{9,11},{10,... | collective-permute-start | bytes 196616 | tf_op jit(solution)/shard_map/ppermute | solution.py:321
  7.8 5.6 %collective-permute-start.10 = (bf16[32,1024]{1,0:T(8,128)(2,1)S(1)}, bf16[32,1024]{1,0:T(8,128)(2,1)S(1)}, u32[]{:S(2)}, u32[]{:S(2)}) collective-permute-start(bf16[32,1024]{1,0:T(8,128)(2,1)S(1)} %attend.3.refs_0_.second_ref), channel_id=1, source_target_pairs={{0,2},{1,3},{2,0},{3,1},{4,6},{5,7},{6,4},{7,5},{8,10},{9,11},{10,... | collective-permute-start | bytes 196616 | tf_op jit(solution)/shard_map/ppermute | solution.py:321
  7.9 7.4 %collective-permute-start.8 = (bf16[32,1024]{1,0:T(8,128)(2,1)S(1)}, bf16[32,1024]{1,0:T(8,128)(2,1)S(1)}, u32[]{:S(2)}, u32[]{:S(2)}) collective-permute-start(bf16[32,1024]{1,0:T(8,128)(2,1)S(1)} %attend.3.refs_0_.second_ref), channel_id=1, source_target_pairs={{0,1},{1,0},{2,3},{3,2},{4,5},{5,4},{6,7},{7,6},{8,9},{9,8},{10,11... | collective-permute-start | bytes 196616 | tf_op jit(solution)/shard_map/ppermute | solution.py:321
  9.8 5.5 %collective-permute-start.1 = (bf16[32,1024]{1,0:T(8,128)(2,1)S(1)}, bf16[32,1024]{1,0:T(8,128)(2,1)S(1)}, u32[]{:S(2)}, u32[]{:S(2)}) collective-permute-start(bf16[32,1024]{1,0:T(8,128)(2,1)S(1)} %get-tuple-element.20.refs_0_.first_ref), channel_id=1, source_target_pairs={{0,1},{1,0},{2,3},{3,2},{4,5},{5,4},{6,7},{7,6},{8,9},{9,8},{10,11... | collective-permute-start | bytes 196616 | tf_op jit(solution)/shard_map/ppermute | solution.py:321
  10.0 6.3 %collective-permute-start.5 = (bf16[32,1024]{1,0:T(8,128)(2,1)S(1)}, bf16[32,1024]{1,0:T(8,128)(2,1)S(1)}, u32[]{:S(2)}, u32[]{:S(2)}) collective-permute-start(bf16[32,1024]{1,0:T(8,128)(2,1)S(1)} %collective-permute-done.3.refs_4_), channel_id=1, source_target_pairs={{0,1},{1,0},{2,3},{3,2},{4,5},{5,4},{6,7},{7,6},{8,9},{9,8},{10,11... | collective-permute-start | bytes 196616 | tf_op jit(solution)/shard_map/ppermute | solution.py:321
  12.2 4.0 %collective-permute-start = (bf16[32,1024]{1,0:T(8,128)(2,1)S(1)}, bf16[32,1024]{1,0:T(8,128)(2,1)S(1)}, u32[]{:S(2)}, u32[]{:S(2)}) collective-permute-start(bf16[32,1024]{1,0:T(8,128)(2,1)S(1)} %get-tuple-element.20.refs_0_.first_ref), channel_id=1, source_target_pairs={{0,4},{4,0},{1,5},{5,1},{2,6},{6,2},{3,7},{7,3},{8,12},{12,8},{9,1... | collective-permute-start | bytes 196616 | tf_op jit(solution)/shard_map/ppermute | solution.py:317
  13.4 4.3 %collective-permute-start.12 = (bf16[32,1024]{1,0:T(8,128)(2,1)S(1)}, bf16[32,1024]{1,0:T(8,128)(2,1)S(1)}, u32[]{:S(2)}, u32[]{:S(2)}) collective-permute-start(bf16[32,1024]{1,0:T(8,128)(2,1)S(1)} %collective-permute-done.10.refs_4_), channel_id=1, source_target_pairs={{0,1},{1,0},{2,3},{3,2},{4,5},{5,4},{6,7},{7,6},{8,9},{9,8},{10,11... | collective-permute-start | bytes 196616 | tf_op jit(solution)/shard_map/ppermute | solution.py:321
  15.2 2.5 %collective-permute-start.4 = (bf16[32,1024]{1,0:T(8,128)(2,1)S(1)}, bf16[32,1024]{1,0:T(8,128)(2,1)S(1)}, u32[]{:S(2)}, u32[]{:S(2)}) collective-permute-start(bf16[32,1024]{1,0:T(8,128)(2,1)S(1)} %collective-permute-done.3.refs_4_), channel_id=1, source_target_pairs={{0,4},{4,0},{1,5},{5,1},{2,6},{6,2},{3,7},{7,3},{8,12},{12,8},{9,1... | collective-permute-start | bytes 196616 | tf_op jit(solution)/shard_map/ppermute | solution.py:317
  15.3 3.0 %collective-permute-start.2 = (bf16[32,1024]{1,0:T(8,128)(2,1)S(1)}, bf16[32,1024]{1,0:T(8,128)(2,1)S(1)}, u32[]{:S(2)}, u32[]{:S(2)}) collective-permute-start(bf16[32,1024]{1,0:T(8,128)(2,1)S(1)} %collective-permute-done.1.refs_2_), channel_id=1, source_target_pairs={{0,4},{4,0},{1,5},{5,1},{2,6},{6,2},{3,7},{7,3},{8,12},{12,8},{9,1... | collective-permute-start | bytes 196616 | tf_op jit(solution)/shard_map/ppermute | solution.py:317
  16.2 2.0 %collective-permute-start.6 = (bf16[32,1024]{1,0:T(8,128)(2,1)S(1)}, bf16[32,1024]{1,0:T(8,128)(2,1)S(1)}, u32[]{:S(2)}, u32[]{:S(2)}) collective-permute-start(bf16[32,1024]{1,0:T(8,128)(2,1)S(1)} %collective-permute-done.5.refs_6_), channel_id=1, source_target_pairs={{0,4},{4,0},{1,5},{5,1},{2,6},{6,2},{3,7},{7,3},{8,12},{12,8},{9,1... | collective-permute-start | bytes 196616 | tf_op jit(solution)/shard_map/ppermute | solution.py:317
  16.2 2.4 %collective-permute-start.7 = (bf16[32,1024]{1,0:T(8,128)(2,1)S(1)}, bf16[32,1024]{1,0:T(8,128)(2,1)S(1)}, u32[]{:S(2)}, u32[]{:S(2)}) collective-permute-start(bf16[32,1024]{1,0:T(8,128)(2,1)S(1)} %attend.3.refs_0_.second_ref), channel_id=1, source_target_pairs={{0,4},{4,0},{1,5},{5,1},{2,6},{6,2},{3,7},{7,3},{8,12},{12,8},{9,1... | collective-permute-start | bytes 196616 | tf_op jit(solution)/shard_map/ppermute | solution.py:317
  17.7 1.3 %collective-permute-start.11 = (bf16[32,1024]{1,0:T(8,128)(2,1)S(1)}, bf16[32,1024]{1,0:T(8,128)(2,1)S(1)}, u32[]{:S(2)}, u32[]{:S(2)}) collective-permute-start(bf16[32,1024]{1,0:T(8,128)(2,1)S(1)} %collective-permute-done.10.refs_4_), channel_id=1, source_target_pairs={{0,4},{4,0},{1,5},{5,1},{2,6},{6,2},{3,7},{7,3},{8,12},{12,8},{9,1... | collective-permute-start | bytes 196616 | tf_op jit(solution)/shard_map/ppermute | solution.py:317
  17.7 1.4 %collective-permute-start.9 = (bf16[32,1024]{1,0:T(8,128)(2,1)S(1)}, bf16[32,1024]{1,0:T(8,128)(2,1)S(1)}, u32[]{:S(2)}, u32[]{:S(2)}) collective-permute-start(bf16[32,1024]{1,0:T(8,128)(2,1)S(1)} %collective-permute-done.8.refs_2_), channel_id=1, source_target_pairs={{0,4},{4,0},{1,5},{5,1},{2,6},{6,2},{3,7},{7,3},{8,12},{12,8},{9,1... | collective-permute-start | bytes 196616 | tf_op jit(solution)/shard_map/ppermute | solution.py:317
  18.2 1.3 %collective-permute-start.13 = (bf16[32,1024]{1,0:T(8,128)(2,1)S(1)}, bf16[32,1024]{1,0:T(8,128)(2,1)S(1)}, u32[]{:S(2)}, u32[]{:S(2)}) collective-permute-start(bf16[32,1024]{1,0:T(8,128)(2,1)S(1)} %collective-permute-done.12.refs_6_), channel_id=1, source_target_pairs={{0,4},{4,0},{1,5},{5,1},{2,6},{6,2},{3,7},{7,3},{8,12},{12,8},{9,1... | collective-permute-start | bytes 196616 | tf_op jit(solution)/shard_map/ppermute | solution.py:317
  24.9 1.4 %collective-permute-start.14 = (bf16[1,64,1024]{2,1,0:T(8,128)(2,1)S(1)}, bf16[1,64,1024]{2,1,0:T(8,128)(2,1)S(1)}, u32[]{:S(2)}, u32[]{:S(2)}) collective-permute-start(bf16[1,64,1024]{2,1,0:T(8,128)(2,1)S(1)} %get-tuple-element.28), channel_id=1, source_target_pairs={{0,4},{4,0},{1,5},{5,1},{2,6},{6,2},{3,7},{7,3},{8,12},{12,8},{9,1... | collective-permute-start | bytes 393224 | tf_op jit(solution)/shard_map/ppermute | solution.py:317
  25.9 3.7 %collective-permute-start.16 = (bf16[1,64,1024]{2,1,0:T(8,128)(2,1)S(1)}, bf16[1,64,1024]{2,1,0:T(8,128)(2,1)S(1)}, u32[]{:S(2)}, u32[]{:S(2)}) collective-permute-start(bf16[1,64,1024]{2,1,0:T(8,128)(2,1)S(1)} %get-tuple-element.32), channel_id=1, source_target_pairs={{0,4},{4,0},{1,5},{5,1},{2,6},{6,2},{3,7},{7,3},{8,12},{12,8},{9,1... | collective-permute-start | bytes 393224 | tf_op jit(solution)/shard_map/ppermute | solution.py:317
  26.4 5.7 %collective-permute-start.17 = (bf16[64,1024]{1,0:T(8,128)(2,1)S(1)}, bf16[64,1024]{1,0:T(8,128)(2,1)S(1)}, u32[]{:S(2)}, u32[]{:S(2)}) collective-permute-start(bf16[64,1024]{1,0:T(8,128)(2,1)S(1)} %fold.3.refs_0_), channel_id=1, source_target_pairs={{0,1},{1,0},{2,3},{3,2},{4,5},{5,4},{6,7},{7,6},{8,9},{9,8},{10,11... | collective-permute-start | bytes 393224 | tf_op jit(solution)/shard_map/ppermute | solution.py:321
  29.5 5.3 %collective-permute-start.15 = (bf16[2,64,1024]{2,1,0:T(8,128)(2,1)S(1)}, bf16[2,64,1024]{2,1,0:T(8,128)(2,1)S(1)}, u32[]{:S(2)}, u32[]{:S(2)}) collective-permute-start(bf16[2,64,1024]{2,1,0:T(8,128)(2,1)S(1)} %get-tuple-element.30), channel_id=1, source_target_pairs={{0,4},{4,0},{1,5},{5,1},{2,6},{6,2},{3,7},{7,3},{8,12},{12,8},{9,1... | collective-permute-start | bytes 786440 | tf_op jit(solution)/shard_map/ppermute | solution.py:317
  32.1 8.6 %collective-permute-start.19 = (bf16[64,1024]{1,0:T(8,128)(2,1)S(1)}, bf16[64,1024]{1,0:T(8,128)(2,1)S(1)}, u32[]{:S(2)}, u32[]{:S(2)}) collective-permute-start(bf16[64,1024]{1,0:T(8,128)(2,1)S(1)} %fold.4.refs_2_), channel_id=1, source_target_pairs={{0,2},{1,3},{2,0},{3,1},{4,6},{5,7},{6,4},{7,5},{8,10},{9,11},{10,... | collective-permute-start | bytes 393224 | tf_op jit(solution)/shard_map/ppermute | solution.py:321
  34.8 6.1 %collective-permute-start.18 = (bf16[64,1024]{1,0:T(8,128)(2,1)S(1)}, bf16[64,1024]{1,0:T(8,128)(2,1)S(1)}, u32[]{:S(2)}, u32[]{:S(2)}) collective-permute-start(bf16[64,1024]{1,0:T(8,128)(2,1)S(1)} %get-tuple-element.34), channel_id=1, source_target_pairs={{0,1},{1,0},{2,3},{3,2},{4,5},{5,4},{6,7},{7,6},{8,9},{9,8},{10,11... | collective-permute-start | bytes 393224 | tf_op jit(solution)/shard_map/ppermute | solution.py:321
  (1 other events, 18.3 us)

commit v2 on v1

v2 whole, which is shorter than its diff:
```python
import functools

import jax
import jax.numpy as jnp
from jax import lax
from jax.experimental import pallas as pl
from jax.experimental.pallas import tpu as pltpu
from jax.sharding import PartitionSpec as P

KV_HEADS = 4
MIB = 1 << 20
LONG = 20000000000
ATTC = 3 * LONG
RELC = 0
STAGEC = 1000000000
DOWNC = 10000000000
SLIM = 4
LOG2E = 1.4426950408889634
VMEM = pl.BlockSpec(memory_space=pltpu.VMEM)
HBM = pl.BlockSpec(memory_space=pltpu.HBM)


def params(limit=1 * MIB):
    return pltpu.CompilerParams(vmem_limit_bytes=limit)


def in_hbm(x):
    return pltpu.with_memory_space_constraint(x, pltpu.HBM)


def cost(flops, bytes_accessed):
    return pl.CostEstimate(flops=flops, bytes_accessed=bytes_accessed, transcendentals=0)


def peer(offset):
    return lax.axis_index("dev") ^ offset


def head_start(offset, width):
    return pl.multiple_of(lax.rem(peer(offset), KV_HEADS) * width, width)


def block_start(devices, offset, rows):
    if devices == KV_HEADS:
        return 0
    return pl.multiple_of(peer(offset) // KV_HEADS * rows, rows)


def column_tiles(units, tile=256):
    return [slice(c, min(c + tile, units)) for c in range(0, units, tile)]


def attend_kernel(devices, len_in, q_in, k_in, v_in, kn_in, vn_in, res_in, out_ref, *scratch):
    len_ref, q_ref, k_ref, v_ref, kn_ref, vn_ref, res_ref, len_sem, small_sem, cache_sem = scratch
    rows, width = q_ref.shape
    head = kn_ref.shape[-1]
    heads = width // head
    cache = k_ref.shape[0] // rows
    halves = cache_sem.shape[1]
    part = rows // halves
    groups = part // 8
    block = lax.axis_index("dev") // KV_HEADS if devices > KV_HEADS else 0
    per_batch = len_ref.shape[-1]
    factor = head ** (-0.5) * LOG2E

    lengths = pltpu.make_async_copy(len_in, len_ref, len_sem)
    small = [
        pltpu.make_async_copy(source, target, small_sem.at[n])
        for n, (source, target) in enumerate(((q_in, q_ref), (kn_in, kn_ref), (vn_in, vn_ref), (res_in, res_ref)))
    ]
    cached = []
    for h in range(halves):
        span = pl.ds(h * part * cache, part * cache)
        cached.append(
            [
                pltpu.make_async_copy(source.at[span], target.at[span], cache_sem.at[n, h])
                for n, (source, target) in enumerate(((k_in, k_ref), (v_in, v_ref)))
            ]
        )
    lengths.start()
    small[0].start()
    small[1].start()
    for pair in cached:
        for copy in pair:
            copy.start()
    small[2].start()
    small[3].start()

    relative = lax.broadcasted_iota(jnp.int32, (8, 8 * cache), 1)
    relative = relative - cache * lax.broadcasted_iota(jnp.int32, (8, 8 * cache), 0)
    relative = jnp.where(relative < 0, cache, relative)
    sub = lax.broadcasted_iota(jnp.int32, (8, 128), 0)
    lengths.wait()
    small[0].wait()
    small[1].wait()
    for h in range(halves):
        stripe = slice(h * part, (h + 1) * part)
        wide = q_ref[stripe, :].astype(jnp.float32)
        fresh_keys = kn_ref[stripe, :].astype(jnp.float32)
        spread, keys_spread, biases = [], [], []
        for g in range(groups):
            own = slice(8 * g, 8 * g + 8)
            spread += [wide[own, i * head : (i + 1) * head] for i in range(heads)]
            keys_spread += [fresh_keys[own]] * heads
            limit = jnp.zeros((8, 128), jnp.int32)
            for r in range(8):
                row = h * part + 8 * g + r
                limit = jnp.where(sub == r, len_ref[block, row // per_batch, row % per_batch], limit)
            limit = jnp.concatenate([limit] * (8 * cache // 128), axis=1)
            bias = jnp.where(relative < limit, 0.0, -1e30)
            biases.append(jnp.concatenate([bias] * heads, axis=0))
        q = jnp.concatenate(spread, axis=0)
        fresh = jnp.sum(q * jnp.concatenate(keys_spread, axis=0), axis=-1, keepdims=True)
        q = q.astype(jnp.bfloat16)
        if h == 0:
            small[2].wait()
            small[3].wait()
        for copy in cached[h]:
            copy.wait()
        scores = []
        span = 8 * cache
        for g in range(groups):
            first = (h * groups + g) * span
            scores.append(
                lax.dot_general(
                    q[8 * heads * g : 8 * heads * (g + 1)],
                    k_ref[first : first + span, :],
                    (((1,), (1,)), ((), ())),
                    preferred_element_type=jnp.float32,
                )
                + biases[g]
            )
        scores = jnp.concatenate(scores, axis=0)
        top = jnp.maximum(jnp.max(scores, axis=-1, keepdims=True), fresh)
        weights = jnp.exp2((scores - top) * factor)
        own_weight = jnp.exp2((fresh - top) * factor)
        inverse = 1.0 / (jnp.sum(weights, axis=-1, keepdims=True) + own_weight)
        own_weight = own_weight * inverse
        weights = weights.astype(jnp.bfloat16)
        for g in range(groups):
            first = (h * groups + g) * span
            block_rows = slice(8 * heads * g, 8 * heads * (g + 1))
            attended = jnp.dot(
                weights[block_rows], v_ref[first : first + span, :], preferred_element_type=jnp.float32
            )
            attended = attended * inverse[block_rows]
            own = slice(h * part + 8 * g, h * part + 8 * g + 8)
            fresh_values = vn_ref[h * part : (h + 1) * part, :].astype(jnp.float32)[8 * g : 8 * g + 8]
            attended = attended + own_weight[block_rows] * jnp.concatenate([fresh_values] * heads, axis=0)
            spread[g] = jnp.concatenate([attended[8 * i : 8 * i + 8] for i in range(heads)], axis=1)
        attended = jnp.concatenate(spread[:groups], axis=0)
        out_ref[stripe, :] = (res_ref[stripe, :].astype(jnp.float32) + attended).astype(out_ref.dtype)


def attend(devices, lengths, *arrays):
    query, keys = arrays[:2]
    rows, width = query.shape
    halves = 2
    return pl.pallas_call(
        functools.partial(attend_kernel, devices),
        out_shape=pltpu.VMEM((rows, width), jnp.bfloat16),
        in_specs=[HBM] * (1 + len(arrays)),
        out_specs=VMEM,
        scratch_shapes=[pltpu.SMEM(lengths.shape, lengths.dtype)]
        + [pltpu.VMEM(a.shape, a.dtype) for a in arrays]
        + [
            pltpu.SemaphoreType.DMA,
            pltpu.SemaphoreType.DMA((4,)),
            pltpu.SemaphoreType.DMA((2, halves)),
        ],
        compiler_params=params(5 * MIB),
        cost_estimate=cost(ATTC, 0),
        name="attend",
    )(lengths, *arrays)


def silu_product(gate, up):
    return (gate / (1.0 + jnp.exp(-gate)) * up).astype(jnp.bfloat16)


def stage_kernel(devices, offsets, first, last, gain_ref, wg_ref, wu_ref, *refs):
    pieces, refs = refs[: 2 * len(offsets)], refs[2 * len(offsets) :]
    if not first:
        gate_in, up_in, square_in = refs[:3]
        refs = refs[3:]
    if last:
        hidden_ref, x_ref = refs[-2:]
    else:
        gate_out, up_out, square_out, x_ref = refs
    rows, width = pieces[0].shape
    units = wg_ref.shape[1]
    many = devices > KV_HEADS
    if many and first:
        for ref in (gate_out, up_out, square_out):
            ref[...] = jnp.zeros_like(ref)
    if many and last:
        gate_out, up_out, square_out = gate_in, up_in, square_in
    if many:
        gate_in, up_in, square_in = gate_out, up_out, square_out
    places, squares = [], []
    for n, offset in enumerate(offsets):
        depth = pl.ds(head_start(offset, width), width)
        places.append((pl.ds(block_start(devices, offset, 2 * rows), 2 * rows), depth))
        gain = gain_ref[depth].astype(jnp.float32).reshape(1, width)
        sums = []
        for side in range(2):
            x = pieces[2 * n + side][...].astype(jnp.float32)
            x_ref[n, side * rows : (side + 1) * rows, :] = (x * gain).astype(jnp.bfloat16)
            sums.append(jnp.sum(x * x, axis=-1, keepdims=True))
        squares.append(jnp.broadcast_to(jnp.concatenate(sums, axis=0), (2 * rows, 128)))

    def product(n, weight, lanes):
        return jnp.dot(x_ref[n], weight[places[n][1], lanes], preferred_element_type=jnp.float32)

    if many:
        for n in range(len(offsets)):
            mine = places[n][0]
            square_out[mine, :] += squares[n]
            for lanes in column_tiles(units):
                gate_out[mine, lanes] += product(n, wg_ref, lanes)
                up_out[mine, lanes] += product(n, wu_ref, lanes)
        if last:
            inverse = lax.rsqrt(square_in[:, :1] / (KV_HEADS * width) + 1e-05)
            for lanes in column_tiles(units):
                hidden_ref[:, lanes] = silu_product(gate_in[:, lanes] * inverse, up_in[:, lanes] * inverse)
        return
    square = sum(squares[1:], squares[0])
    if not first:
        square = square + square_in[...]
    if last:
        inverse = lax.rsqrt(square[:, :1] / (KV_HEADS * width) + 1e-05)
    else:
        square_out[...] = square
    for lanes in column_tiles(units):
        gate = sum(product(n, wg_ref, lanes) for n in range(len(offsets)))
        up = sum(product(n, wu_ref, lanes) for n in range(len(offsets)))
        if not first:
            gate = gate + gate_in[:, lanes]
            up = up + up_in[:, lanes]
        if last:
            hidden_ref[:, lanes] = silu_product(gate * inverse, up * inverse)
        else:
            gate_out[:, lanes] = gate
            up_out[:, lanes] = up


def stage(devices, offsets, pieces, gain, w_gate, w_up, state, final, present):
    rows, width = pieces[0].shape
    units = w_gate.shape[1]
    total = devices // KV_HEADS * 2 * rows
    first, last = not state, final
    arguments = [gain, w_gate, w_up] + list(pieces) + list(state)
    if final:
        arguments += present
    aliases = {}
    if last:
        shapes = [pltpu.VMEM((total, units), jnp.bfloat16)]
    else:
        shapes = [
            pltpu.VMEM((total, units), jnp.float32),
            pltpu.VMEM((total, units), jnp.float32),
            pltpu.VMEM((total, 128), jnp.float32),
        ]
        if not first:
            aliases = {len(arguments) - 3 + n: n for n in range(3)}
    return pl.pallas_call(
        functools.partial(stage_kernel, devices, offsets, first, last),
        out_shape=shapes,
        in_specs=[VMEM] * len(arguments),
        out_specs=[VMEM] * len(shapes),
        input_output_aliases=aliases,
        scratch_shapes=[pltpu.VMEM((len(offsets), 2 * rows, width), jnp.bfloat16)],
        compiler_params=params(devices // KV_HEADS * SLIM * MIB),
        cost_estimate=cost(STAGEC, 0),
        name="stage",
    )(*arguments)


def relay_kernel(piece_ref, *refs):
    refs[-1][...] = piece_ref[...]


def relay(piece, after, present):
    return pl.pallas_call(
        relay_kernel,
        out_shape=pltpu.VMEM(piece.shape, piece.dtype),
        in_specs=[VMEM] + [pl.BlockSpec(memory_space=pl.ANY)] * len(after) + [VMEM] * len(present),
        out_specs=VMEM,
        compiler_params=params(),
        cost_estimate=cost(RELC, 0),
        name="relay",
    )(piece, *after, *present)


def down_kernel(devices, offsets, hidden_ref, weight_ref, *refs):
    keep_ref, send_ref = refs[-2:]
    _, rows, width = keep_ref.shape
    for n, offset in enumerate(offsets):
        mine = pl.ds(block_start(devices, offset, 2 * rows), 2 * rows)
        hidden = hidden_ref[mine, :]
        for lanes in column_tiles(width):
            size = lanes.stop - lanes.start
            column = pl.multiple_of(head_start(offset, width) + lanes.start, size)
            term = jnp.dot(hidden, weight_ref[:, pl.ds(column, size)], preferred_element_type=jnp.float32)
            keep_ref[n, :, lanes] = term[:rows]
            send_ref[n, :, lanes] = term[rows:].astype(jnp.bfloat16)


def down(devices, offsets, hidden, w_down, rows, after=()):
    units, features = w_down.shape
    width = features // KV_HEADS
    shape = (len(offsets), rows, width)
    return pl.pallas_call(
        functools.partial(down_kernel, devices, offsets),
        out_shape=[pltpu.VMEM(shape, jnp.float32), pltpu.VMEM(shape, jnp.bfloat16)],
        in_specs=[VMEM] * 2 + [pl.BlockSpec(memory_space=pl.ANY)] * len(after),
        out_specs=[VMEM] * 2,
        compiler_params=params(),
        cost_estimate=cost(DOWNC, 0),
        name="down",
    )(hidden, w_down, *after)


def fold_kernel(offsets, count, *refs):
    keep_ref, got_ref = refs[:2]
    more, out_refs = refs[2 : 2 + count], refs[-len(offsets) :]
    for n, out_ref in enumerate(out_refs):
        term = keep_ref[n] + got_ref[n].astype(jnp.float32)
        for ref in more:
            term = term + ref[...].astype(jnp.float32)
        out_ref[...] = term.astype(out_ref.dtype)


def fold(offsets, keep, got, more=(), after=(), flops=0):
    _, rows, width = keep.shape
    return pl.pallas_call(
        functools.partial(fold_kernel, offsets, len(more)),
        out_shape=[pltpu.VMEM((rows, width), jnp.float32 if o == 0 else jnp.bfloat16) for o in offsets],
        in_specs=[VMEM] * (2 + len(more)) + [pl.BlockSpec(memory_space=pl.ANY)] * len(after),
        out_specs=[VMEM] * len(offsets),
        compiler_params=params(),
        cost_estimate=cost(flops, 0),
        name="fold",
    )(keep, got, *more, *after)


def finish_kernel(stream_ref, *refs):
    out_ref = refs[-1]
    total = stream_ref[...].astype(jnp.float32)
    for ref in refs[:-1]:
        total = total + ref[...].astype(jnp.float32)
    out_ref[...] = total.astype(out_ref.dtype)


def finish(stream, terms):
    return pl.pallas_call(
        finish_kernel,
        out_shape=jax.ShapeDtypeStruct(stream.shape, jnp.bfloat16),
        compiler_params=params(),
        name="finish",
    )(stream, *terms)


def swap(x):
    return lax.ppermute(x, "att", [(0, 1), (1, 0)])


def exchange(x, offset, devices):
    return lax.ppermute(x, "dev", [(i, i ^ offset) for i in range(devices)])


def shards(
    query, key_cache, value_cache, key_new, value_new, lengths, resid, gain, w_gate, w_up, w_down
):
    devices = lax.axis_size("dev")
    width = query.shape[-1]
    head = key_cache.shape[-1]
    stream = attend(
        devices,
        in_hbm(lengths[0]),
        in_hbm(query.reshape(-1, width)),
        in_hbm(key_cache.reshape(-1, head)),
        in_hbm(value_cache.reshape(-1, head)),
        in_hbm(key_new.reshape(-1, head)),
        in_hbm(value_new.reshape(-1, head)),
        in_hbm(resid.reshape(-1, width)),
    )
    rows = stream.shape[0]
    pieces = {0: stream}
    bit = devices // 2
    while bit:
        for o in tuple(pieces):
            pieces[o ^ bit] = exchange(pieces[o], bit, devices)
        bit //= 2
    groups = [(0,), (2, 1), (3,)] if devices == 4 else [(o,) for o in range(devices)]
    state = ()
    for group in groups:
        arrived = []
        for o in group:
            piece = pieces[o]
            if state and group is groups[-1]:
                piece = relay(piece, state[2:], [w_down])
            elif state:
                piece = relay(piece, state[2:], [])
            arrived += [piece, swap(piece)]
        state = stage(devices, group, arrived, gain, w_gate, w_up, state, group is groups[-1], [])
    hidden = state[0]

    def part(offsets, after=()):
        keep, send = down(devices, offsets, hidden, w_down, rows, after)
        return offsets, keep, swap(send)

    if devices == 4:
        (third,) = fold(*part((3,)))
        relayed = exchange(third, 1, devices)
        second_parts = part((2,))
        nearer_parts = part((1, 0), (third,))
        (second,) = fold(*second_parts, (relayed,), (), LONG)
        first, own = fold(*nearer_parts, (), (second,))
        terms = [own, exchange(first, 1, devices), exchange(second, 2, devices)]
    else:
        terms = {}
        for start in range(devices - 2, -1, -2):
            offsets = (start + 1, start)
            for o, term in zip(offsets, fold(*part(offsets))):
                terms[o] = term if o == 0 else exchange(term, o, devices)
        terms = [terms[o] for o in range(devices)]
    return finish(stream, terms).reshape(query.shape)


def solution(mesh):
    return jax.shard_map(
        shards,
        mesh=mesh,
        in_specs=(
            P(("grp", "att"), "dev", None, None, None),
            P(("grp", "att"), "dev", None, None, None, None),
            P(("grp", "att"), "dev", None, None, None, None),
            P(("grp", "att"), "dev", None, None, None),
            P(("grp", "att"), "dev", None, None, None),
            P(("grp", "att"), None, None, None),
            P(("grp", "att"), "dev", None, None, None),
            P(),
            P(None, ("att", "dev")),
            P(None, ("att", "dev")),
            P(("att", "dev"), None),
        ),
        out_specs=P(("grp", "att"), "dev", None, None, None),
        check_vma=False,
    )
```

time: 41.9 us -> 40.6 us (0.969)
  starting transfers between devices: 18.8 us -> 14 us
  waiting for transfers between devices: 10.5 us -> 13.4 us
  local copies, waits for them, and re-layouts: 0.06 us -> 1.38 us
    ppermute x9 -> x6, starting transfers between devices: 16.5 us -> 12.1 us  [exchange(): return lax.ppermute(x, 'dev', [(i, i ^ offset) for i in range(devices)])]
    ppermute x9 -> x6, waiting for transfers between devices: 9.56 us -> 12 us  [exchange(): return lax.ppermute(x, 'dev', [(i, i ^ offset) for i in range(devices)])]
    unnamed x26 -> x14, local copies, waits for them, and re-layouts: 0.06 us -> 1.38 us
    ppermute x11 -> x7, waiting for transfers between devices: 0.92 us -> 1.41 us  [swap(): return lax.ppermute(x, 'att', [(0, 1), (1, 0)])]
    ppermute x11 -> x7, starting transfers between devices: 2.3 us -> 1.85 us  [swap(): return lax.ppermute(x, 'att', [(0, 1), (1, 0)])]
    pallas_call x5 -> x8, Pallas kernels: 9.17 us -> 8.81 us  [the longest x3 5.09 us: stage(): pl.pallas_call(functools.partial(stage_kernel, devices, offsets, first, l...]
  transfers between devices with their start and end apart: 20 -> 13, of which waited for: 10 -> 8; matrix products, arithmetic and copies ran while one was open for 0% -> 0% of each run, Pallas kernels for 9% -> 14%
where the time goes in v2:
time: 40.6 us; the launch traced here: 40.5 us
  starting transfers between devices  14 us (34%)
  waiting for transfers between devices  13.4 us (33%)
  Pallas kernels  11.6 us (29%)
  local copies, waits for them, and re-layouts  1.38 us (3%)
    ppermute x6, starting transfers between devices, exchange(): return lax.ppermute(x, 'dev', [(i, i ^ offset) for i in range(devices)])  12.1 us
    ppermute x6, waiting for transfers between devices, exchange(): return lax.ppermute(x, 'dev', [(i, i ^ offset) for i in range(devices)])  12 us
    pallas_call x3, Pallas kernels, stage(): pl.pallas_call(functools.partial(stage_kernel, devices, offsets, first, l...  5.09 us
    pallas_call x1, Pallas kernels, attend(): pl.pallas_call(functools.partial(attend_kernel, devices), out_shape=pltpu...  2.97 us
    pallas_call x3, Pallas kernels, down(): pl.pallas_call(functools.partial(down_kernel, devices, offsets), out_shap...  2.64 us
    ppermute x7, starting transfers between devices, swap(): return lax.ppermute(x, 'att', [(0, 1), (1, 0)])  1.85 us
    ppermute x7, waiting for transfers between devices, swap(): return lax.ppermute(x, 'att', [(0, 1), (1, 0)])  1.41 us
    unnamed x14, local copies, waits for them, and re-layouts  1.38 us
  transfers between devices with their start and end apart: 13, of which 8 were waited for; matrix products, arithmetic and copies ran while one was open for 0% of the time, Pallas kernels for 14%

profile of v2, /device:TPU:0, one launch (start us, length us, event | category | flops | bytes accessed | tf_op | source)
XLA Modules:
  0.0 40.5 jit_solution(11796348871936799626)
XLA Ops:
  0.0 3.0 %attend.1.refs_0_.stream_ref = bf16[64,1024]{1,0:T(8,128)(2,1)S(1)} custom-call(s32[1,2,32]{2,1,0:T(2,128)} %bitcast.16, bf16[64,1024]{1,0:T(8,128)(2,1)} %bitcast.12, bf16[4096,128]{1,0:T(8,128)(2,1)} %bitcast.10, bf16[4096,128]{1,0:T(8,128)(2,1)} %bitcast.11, bf16[64,128]{1,0:T(8,128)(2,1)} %bitcast.14, bf16[64,128]{1,0:T(8,128)(2,1)} %bitcast.15, ...), custom_call_target="tpu_custom_call" | custom-call | flops 60000002048 | tf_op jit(solution)/shard_map/attend/pallas_call | solution.py:159
  3.0 0.5 %collective-permute-start.2 = (bf16[64,1024]{1,0:T(8,128)(2,1)S(1)}, bf16[64,1024]{1,0:T(8,128)(2,1)S(1)}, u32[]{:S(2)}, u32[]{:S(2)}) collective-permute-start(bf16[64,1024]{1,0:T(8,128)(2,1)S(1)} %attend.1.refs_0_.stream_ref), channel_id=1, source_target_pairs={{0,4},{4,0},{1,5},{5,1},{2,6},{6,2},{3,7},{7,3},{8,12},{12,8},{9,1... | collective-permute-start | bytes 393224 | tf_op jit(solution)/shard_map/ppermute | solution.py:365
  3.5 3.7 %collective-permute-start = (bf16[64,1024]{1,0:T(8,128)(2,1)S(1)}, bf16[64,1024]{1,0:T(8,128)(2,1)S(1)}, u32[]{:S(2)}, u32[]{:S(2)}) collective-permute-start(bf16[64,1024]{1,0:T(8,128)(2,1)S(1)} %attend.1.refs_0_.stream_ref), channel_id=1, source_target_pairs={{0,2},{1,3},{2,0},{3,1},{4,6},{5,7},{6,4},{7,5},{8,10},{9,11},{10,... | collective-permute-start | bytes 393224 | tf_op jit(solution)/shard_map/ppermute | solution.py:369
  7.2 1.6 %collective-permute-start.4 = (bf16[64,1024]{1,0:T(8,128)(2,1)S(1)}, bf16[64,1024]{1,0:T(8,128)(2,1)S(1)}, u32[]{:S(2)}, u32[]{:S(2)}) collective-permute-start(bf16[64,1024]{1,0:T(8,128)(2,1)S(1)} %attend.1.refs_0_.stream_ref), channel_id=1, source_target_pairs={{0,1},{1,0},{2,3},{3,2},{4,5},{5,4},{6,7},{7,6},{8,9},{9,8},{10,11... | collective-permute-start | bytes 393224 | tf_op jit(solution)/shard_map/ppermute | solution.py:369
  8.8 1.4 %copy-done.1 = bf16[4096,1792]{1,0:T(8,128)(2,1)S(1)} copy-done((bf16[4096,1792]{1,0:T(8,128)(2,1)S(1)}, bf16[4096,1792]{1,0:T(8,128)(2,1)}, u32[]{:S(2)}) %copy-start.1) | copy-done | bytes 14680088
  10.1 1.2 %stage.3 = (f32[128,1792]{1,0:T(8,128)S(1)}, f32[128,1792]{1,0:T(8,128)S(1)}, f32[128,128]{1,0:T(8,128)S(1)}) custom-call(bf16[4096]{0:T(1024)(128)(2,1)S(1)} %copy-done.2, bf16[4096,1792]{1,0:T(8,128)(2,1)S(1)} %copy-done, bf16[4096,1792]{1,0:T(8,128)(2,1)S(1)} %copy-done.1, bf16[64,1024]{1,0:T(8,128)(2,1)S(1)} %attend.1.refs_0_.stream_ref, ...), custom_call_target="tpu_custom_call" | custom-call | flops 1000000000 | tf_op jit(solution)/shard_map/stage/pallas_call | solution.py:266
  11.3 2.9 %collective-permute-done.piece_ref = bf16[64,1024]{1,0:T(8,128)(2,1)S(1)} collective-permute-done((bf16[64,1024]{1,0:T(8,128)(2,1)S(1)}, bf16[64,1024]{1,0:T(8,128)(2,1)S(1)}, u32[]{:S(2)}, u32[]{:S(2)}) %collective-permute-start) | collective-permute-done | bytes 131104 | tf_op jit(solution)/shard_map/ppermute | solution.py:369
  14.2 0.1 collective-permute-start.3
  14.3 0.1 collective-permute-done.4.piece_ref
  14.4 0.5 %collective-permute-start.5 = (bf16[64,1024]{1,0:T(8,128)(2,1)S(1)}, bf16[64,1024]{1,0:T(8,128)(2,1)S(1)}, u32[]{:S(2)}, u32[]{:S(2)}) collective-permute-start(bf16[64,1024]{1,0:T(8,128)(2,1)S(1)} %relay.4.refs_2_), channel_id=1, source_target_pairs={{0,4},{4,0},{1,5},{5,1},{2,6},{6,2},{3,7},{7,3},{8,12},{12,8},{9,1... | collective-permute-start | bytes 393224 | tf_op jit(solution)/shard_map/ppermute | solution.py:365
  14.8 1.2 %collective-permute-start.1 = (bf16[64,1024]{1,0:T(8,128)(2,1)S(1)}, bf16[64,1024]{1,0:T(8,128)(2,1)S(1)}, u32[]{:S(2)}, u32[]{:S(2)}) collective-permute-start(bf16[64,1024]{1,0:T(8,128)(2,1)S(1)} %collective-permute-done.piece_ref), channel_id=1, source_target_pairs={{0,1},{1,0},{2,3},{3,2},{4,5},{5,4},{6,7},{7,6},{8,9},{9,8},{10,11... | collective-permute-start | bytes 393224 | tf_op jit(solution)/shard_map/ppermute | solution.py:369
  16.0 0.0 collective-permute-done.3.refs_1_
  16.0 0.0 collective-permute-done.5.refs_3_
  16.0 2.5 %stage.4 = (f32[128,1792]{1,0:T(8,128)S(1)}, f32[128,1792]{1,0:T(8,128)S(1)}, f32[128,128]{1,0:T(8,128)S(1)}) custom-call(bf16[4096]{0:T(1024)(128)(2,1)S(1)} %copy-done.2, bf16[4096,1792]{1,0:T(8,128)(2,1)S(1)} %copy-done, bf16[4096,1792]{1,0:T(8,128)(2,1)S(1)} %copy-done.1, ...), custom_call_target="tpu_custom_call", output_to_operand_aliasing={{0}: (7, {}), {1}: (8, {}), {2}: (9, {})} | custom-call | flops 1000000000 | tf_op jit(solution)/shard_map/stage/pallas_call | solution.py:266
  18.6 1.8 %collective-permute-done.1.piece_ref = bf16[64,1024]{1,0:T(8,128)(2,1)S(1)} collective-permute-done((bf16[64,1024]{1,0:T(8,128)(2,1)S(1)}, bf16[64,1024]{1,0:T(8,128)(2,1)S(1)}, u32[]{:S(2)}, u32[]{:S(2)}) %collective-permute-start.1) | collective-permute-done | bytes 131104 | tf_op jit(solution)/shard_map/ppermute | solution.py:369
  20.4 0.1 collective-permute-start.6
  20.5 1.3 %collective-permute-done.6.refs_1_ = bf16[64,1024]{1,0:T(8,128)(2,1)S(1)} collective-permute-done((bf16[64,1024]{1,0:T(8,128)(2,1)S(1)}, bf16[64,1024]{1,0:T(8,128)(2,1)S(1)}, u32[]{:S(2)}, u32[]{:S(2)}) %collective-permute-start.6) | collective-permute-done | bytes 131104 | tf_op jit(solution)/shard_map/ppermute | solution.py:365
  21.8 1.4 %stage.5.hidden_ref = bf16[128,1792]{1,0:T(8,128)(2,1)S(1)} custom-call(bf16[4096]{0:T(1024)(128)(2,1)S(1)} %copy-done.2, bf16[4096,1792]{1,0:T(8,128)(2,1)S(1)} %copy-done, bf16[4096,1792]{1,0:T(8,128)(2,1)S(1)} %copy-done.1, bf16[64,1024]{1,0:T(8,128)(2,1)S(1)} %relay.5.refs_0_, bf16[64,1024]{1,0:T(8,128)(2,1)S(1)} %collective-permute-done.6.refs_1_, ...), custom_call_target="tpu_custom_call" | custom-call | flops 1000000000 | tf_op jit(solution)/shard_map/stage/pallas_call | solution.py:266
  23.2 0.7 %down.3 = (f32[1,64,1024]{2,1,0:T(8,128)S(1)}, bf16[1,64,1024]{2,1,0:T(8,128)(2,1)S(1)}) custom-call(bf16[128,1792]{1,0:T(8,128)(2,1)S(1)} %stage.5.hidden_ref, bf16[1792,4096]{1,0:T(8,128)(2,1)S(1)} %bitcast.9), custom_call_target="tpu_custom_call" | custom-call | flops 10000000000 | tf_op jit(solution)/shard_map/down/pallas_call | solution.py:313
  23.9 0.2 collective-permute-start.7
  24.1 0.7 %down.5 = (f32[1,64,1024]{2,1,0:T(8,128)S(1)}, bf16[1,64,1024]{2,1,0:T(8,128)(2,1)S(1)}) custom-call(bf16[128,1792]{1,0:T(8,128)(2,1)S(1)} %stage.5.hidden_ref, bf16[1792,4096]{1,0:T(8,128)(2,1)S(1)} %bitcast.9), custom_call_target="tpu_custom_call" | custom-call | flops 10000000000 | tf_op jit(solution)/shard_map/down/pallas_call | solution.py:313
  24.9 0.4 %collective-permute-start.9 = (bf16[1,64,1024]{2,1,0:T(8,128)(2,1)S(1)}, bf16[1,64,1024]{2,1,0:T(8,128)(2,1)S(1)}, u32[]{:S(2)}, u32[]{:S(2)}) collective-permute-start(bf16[1,64,1024]{2,1,0:T(8,128)(2,1)S(1)} %get-tuple-element.30), channel_id=1, source_target_pairs={{0,4},{4,0},{1,5},{5,1},{2,6},{6,2},{3,7},{7,3},{8,12},{12,8},{9,1... | collective-permute-start | bytes 393224 | tf_op jit(solution)/shard_map/ppermute | solution.py:365
  25.3 0.1 collective-permute-done.7.refs_1_
  25.4 1.6 %collective-permute-start.10 = (bf16[64,1024]{1,0:T(8,128)(2,1)S(1)}, bf16[64,1024]{1,0:T(8,128)(2,1)S(1)}, u32[]{:S(2)}, u32[]{:S(2)}) collective-permute-start(bf16[64,1024]{1,0:T(8,128)(2,1)S(1)} %fold.3.refs_0_), channel_id=1, source_target_pairs={{0,1},{1,0},{2,3},{3,2},{4,5},{5,4},{6,7},{7,6},{8,9},{9,8},{10,11... | collective-permute-start | bytes 393224 | tf_op jit(solution)/shard_map/ppermute | solution.py:369
  27.0 1.2 %down.4 = (f32[2,64,1024]{2,1,0:T(8,128)S(1)}, bf16[2,64,1024]{2,1,0:T(8,128)(2,1)S(1)}) custom-call(bf16[128,1792]{1,0:T(8,128)(2,1)S(1)} %stage.5.hidden_ref, bf16[1792,4096]{1,0:T(8,128)(2,1)S(1)} %bitcast.9, bf16[64,1024]{1,0:T(8,128)(2,1)S(1)} %fold.3.refs_0_), custom_call_target="tpu_custom_call" | custom-call | flops 10000000000 | tf_op jit(solution)/shard_map/down/pallas_call | solution.py:313
  28.2 0.1 collective-permute-start.8
  28.3 2.7 %collective-permute-done.10.refs_2_ = bf16[64,1024]{1,0:T(8,128)(2,1)S(1)} collective-permute-done((bf16[64,1024]{1,0:T(8,128)(2,1)S(1)}, bf16[64,1024]{1,0:T(8,128)(2,1)S(1)}, u32[]{:S(2)}, u32[]{:S(2)}) %collective-permute-start.10) | collective-permute-done | bytes 131104 | tf_op jit(solution)/shard_map/ppermute | solution.py:369
  31.0 2.3 %collective-permute-start.12 = (bf16[64,1024]{1,0:T(8,128)(2,1)S(1)}, bf16[64,1024]{1,0:T(8,128)(2,1)S(1)}, u32[]{:S(2)}, u32[]{:S(2)}) collective-permute-start(bf16[64,1024]{1,0:T(8,128)(2,1)S(1)} %fold.4.refs_2_), channel_id=1, source_target_pairs={{0,2},{1,3},{2,0},{3,1},{4,6},{5,7},{6,4},{7,5},{8,10},{9,11},{10,... | collective-permute-start | bytes 393224 | tf_op jit(solution)/shard_map/ppermute | solution.py:369
  33.4 1.8 %collective-permute-start.11 = (bf16[64,1024]{1,0:T(8,128)(2,1)S(1)}, bf16[64,1024]{1,0:T(8,128)(2,1)S(1)}, u32[]{:S(2)}, u32[]{:S(2)}) collective-permute-start(bf16[64,1024]{1,0:T(8,128)(2,1)S(1)} %get-tuple-element.32), channel_id=1, source_target_pairs={{0,1},{1,0},{2,3},{3,2},{4,5},{5,4},{6,7},{7,6},{8,9},{9,8},{10,11... | collective-permute-start | bytes 393224 | tf_op jit(solution)/shard_map/ppermute | solution.py:369
  35.2 4.4 %collective-permute-done.12.refs_2_ = bf16[64,1024]{1,0:T(8,128)(2,1)S(1)} collective-permute-done((bf16[64,1024]{1,0:T(8,128)(2,1)S(1)}, bf16[64,1024]{1,0:T(8,128)(2,1)S(1)}, u32[]{:S(2)}, u32[]{:S(2)}) %collective-permute-start.12) | collective-permute-done | bytes 131104 | tf_op jit(solution)/shard_map/ppermute | solution.py:369
  39.6 0.2 collective-permute-done.11.refs_1_
  39.7 0.7 %finish.1 = bf16[64,1024]{1,0:T(8,128)(2,1)} custom-call(bf16[64,1024]{1,0:T(8,128)(2,1)S(1)} %attend.1.refs_0_.stream_ref, f32[64,1024]{1,0:T(8,128)S(1)} %get-tuple-element.31.refs_0_, bf16[64,1024]{1,0:T(8,128)(2,1)S(1)} %collective-permute-done.11.refs_1_, bf16[64,1024]{1,0:T(8,128)(2,1)S(1)} %collective-permute-done.12.refs_2_), custom_call_target="tpu_custom_call" | custom-call | tf_op jit(solution)/shard_map/finish/pallas_call | solution.py:356
  (23 shorter events, 0.2 us)
Async XLA Ops:
  0.0 8.7 %copy-start = (bf16[4096,1792]{1,0:T(8,128)(2,1)S(1)}, bf16[4096,1792]{1,0:T(8,128)(2,1)}, u32[]{:S(2)}) copy-start(bf16[4096,1792]{1,0:T(8,128)(2,1)} %wg_ref.5) | copy-start | bytes 44040196
  0.0 10.1 %copy-start.1 = (bf16[4096,1792]{1,0:T(8,128)(2,1)S(1)}, bf16[4096,1792]{1,0:T(8,128)(2,1)}, u32[]{:S(2)}) copy-start(bf16[4096,1792]{1,0:T(8,128)(2,1)} %wu_ref.5) | copy-start | bytes 44040196
  0.0 10.1 %copy-start.2 = (bf16[4096]{0:T(1024)(128)(2,1)S(1)}, bf16[4096]{0:T(1024)(128)(2,1)}, u32[]{:S(2)}) copy-start(bf16[4096]{0:T(1024)(128)(2,1)} %gain_ref.5) | copy-start | bytes 24580
  3.0 5.8 %collective-permute-start.2 = (bf16[64,1024]{1,0:T(8,128)(2,1)S(1)}, bf16[64,1024]{1,0:T(8,128)(2,1)S(1)}, u32[]{:S(2)}, u32[]{:S(2)}) collective-permute-start(bf16[64,1024]{1,0:T(8,128)(2,1)S(1)} %attend.1.refs_0_.stream_ref), channel_id=1, source_target_pairs={{0,4},{4,0},{1,5},{5,1},{2,6},{6,2},{3,7},{7,3},{8,12},{12,8},{9,1... | collective-permute-start | bytes 393224 | tf_op jit(solution)/shard_map/ppermute | solution.py:365
  3.5 10.7 %collective-permute-start = (bf16[64,1024]{1,0:T(8,128)(2,1)S(1)}, bf16[64,1024]{1,0:T(8,128)(2,1)S(1)}, u32[]{:S(2)}, u32[]{:S(2)}) collective-permute-start(bf16[64,1024]{1,0:T(8,128)(2,1)S(1)} %attend.1.refs_0_.stream_ref), channel_id=1, source_target_pairs={{0,2},{1,3},{2,0},{3,1},{4,6},{5,7},{6,4},{7,5},{8,10},{9,11},{10,... | collective-permute-start | bytes 393224 | tf_op jit(solution)/shard_map/ppermute | solution.py:369
  7.2 7.2 %collective-permute-start.4 = (bf16[64,1024]{1,0:T(8,128)(2,1)S(1)}, bf16[64,1024]{1,0:T(8,128)(2,1)S(1)}, u32[]{:S(2)}, u32[]{:S(2)}) collective-permute-start(bf16[64,1024]{1,0:T(8,128)(2,1)S(1)} %attend.1.refs_0_.stream_ref), channel_id=1, source_target_pairs={{0,1},{1,0},{2,3},{3,2},{4,5},{5,4},{6,7},{7,6},{8,9},{9,8},{10,11... | collective-permute-start | bytes 393224 | tf_op jit(solution)/shard_map/ppermute | solution.py:369
  10.1 10.2 %slice-start = ((s8[14680064]{0:T(1024)(128)(4,1)}), s8[4194304]{0:T(1024)(128)(4,1)S(1)}, s32[]{:S(2)}) async-start(s8[14680064]{0:T(1024)(128)(4,1)} %bitcast.8), calls=%async_computation | async-start | bytes 8388608
  10.1 10.2 %slice-start.1 = ((s8[14680064]{0:T(1024)(128)(4,1)}), s8[4194304]{0:T(1024)(128)(4,1)S(1)}, s32[]{:S(2)}) async-start(s8[14680064]{0:T(1024)(128)(4,1)} %bitcast.8), calls=%async_computation.1 | async-start | bytes 8388608
  14.2 1.8 %collective-permute-start.3 = (bf16[64,1024]{1,0:T(8,128)(2,1)S(1)}, bf16[64,1024]{1,0:T(8,128)(2,1)S(1)}, u32[]{:S(2)}, u32[]{:S(2)}) collective-permute-start(bf16[64,1024]{1,0:T(8,128)(2,1)S(1)} %relay.3.refs_0_), channel_id=1, source_target_pairs={{0,4},{4,0},{1,5},{5,1},{2,6},{6,2},{3,7},{7,3},{8,12},{12,8},{9,1... | collective-permute-start | bytes 393224 | tf_op jit(solution)/shard_map/ppermute | solution.py:365
  14.4 1.7 %collective-permute-start.5 = (bf16[64,1024]{1,0:T(8,128)(2,1)S(1)}, bf16[64,1024]{1,0:T(8,128)(2,1)S(1)}, u32[]{:S(2)}, u32[]{:S(2)}) collective-permute-start(bf16[64,1024]{1,0:T(8,128)(2,1)S(1)} %relay.4.refs_2_), channel_id=1, source_target_pairs={{0,4},{4,0},{1,5},{5,1},{2,6},{6,2},{3,7},{7,3},{8,12},{12,8},{9,1... | collective-permute-start | bytes 393224 | tf_op jit(solution)/shard_map/ppermute | solution.py:365
  14.8 5.5 %collective-permute-start.1 = (bf16[64,1024]{1,0:T(8,128)(2,1)S(1)}, bf16[64,1024]{1,0:T(8,128)(2,1)S(1)}, u32[]{:S(2)}, u32[]{:S(2)}) collective-permute-start(bf16[64,1024]{1,0:T(8,128)(2,1)S(1)} %collective-permute-done.piece_ref), channel_id=1, source_target_pairs={{0,1},{1,0},{2,3},{3,2},{4,5},{5,4},{6,7},{7,6},{8,9},{9,8},{10,11... | collective-permute-start | bytes 393224 | tf_op jit(solution)/shard_map/ppermute | solution.py:369
  16.0 4.3 %slice-start.2 = ((s8[14680064]{0:T(1024)(128)(4,1)}), s8[4194304]{0:T(1024)(128)(4,1)S(1)}, s32[]{:S(2)}) async-start(s8[14680064]{0:T(1024)(128)(4,1)} %bitcast.8), calls=%async_computation.2 | async-start | bytes 8388608
  16.0 4.3 %slice-start.3 = ((s8[14680064]{0:T(1024)(128)(4,1)}), s8[2097152]{0:T(1024)(128)(4,1)S(1)}, s32[]{:S(2)}) async-start(s8[14680064]{0:T(1024)(128)(4,1)} %bitcast.8), calls=%async_computation.3 | async-start | bytes 4194304
  20.4 1.4 %collective-permute-start.6 = (bf16[64,1024]{1,0:T(8,128)(2,1)S(1)}, bf16[64,1024]{1,0:T(8,128)(2,1)S(1)}, u32[]{:S(2)}, u32[]{:S(2)}) collective-permute-start(bf16[64,1024]{1,0:T(8,128)(2,1)S(1)} %relay.5.refs_0_), channel_id=1, source_target_pairs={{0,4},{4,0},{1,5},{5,1},{2,6},{6,2},{3,7},{7,3},{8,12},{12,8},{9,1... | collective-permute-start | bytes 393224 | tf_op jit(solution)/shard_map/ppermute | solution.py:365
  23.9 1.4 %collective-permute-start.7 = (bf16[1,64,1024]{2,1,0:T(8,128)(2,1)S(1)}, bf16[1,64,1024]{2,1,0:T(8,128)(2,1)S(1)}, u32[]{:S(2)}, u32[]{:S(2)}) collective-permute-start(bf16[1,64,1024]{2,1,0:T(8,128)(2,1)S(1)} %get-tuple-element.26), channel_id=1, source_target_pairs={{0,4},{4,0},{1,5},{5,1},{2,6},{6,2},{3,7},{7,3},{8,12},{12,8},{9,1... | collective-permute-start | bytes 393224 | tf_op jit(solution)/shard_map/ppermute | solution.py:365
  24.9 3.4 %collective-permute-start.9 = (bf16[1,64,1024]{2,1,0:T(8,128)(2,1)S(1)}, bf16[1,64,1024]{2,1,0:T(8,128)(2,1)S(1)}, u32[]{:S(2)}, u32[]{:S(2)}) collective-permute-start(bf16[1,64,1024]{2,1,0:T(8,128)(2,1)S(1)} %get-tuple-element.30), channel_id=1, source_target_pairs={{0,4},{4,0},{1,5},{5,1},{2,6},{6,2},{3,7},{7,3},{8,12},{12,8},{9,1... | collective-permute-start | bytes 393224 | tf_op jit(solution)/shard_map/ppermute | solution.py:365
  25.4 5.6 %collective-permute-start.10 = (bf16[64,1024]{1,0:T(8,128)(2,1)S(1)}, bf16[64,1024]{1,0:T(8,128)(2,1)S(1)}, u32[]{:S(2)}, u32[]{:S(2)}) collective-permute-start(bf16[64,1024]{1,0:T(8,128)(2,1)S(1)} %fold.3.refs_0_), channel_id=1, source_target_pairs={{0,1},{1,0},{2,3},{3,2},{4,5},{5,4},{6,7},{7,6},{8,9},{9,8},{10,11... | collective-permute-start | bytes 393224 | tf_op jit(solution)/shard_map/ppermute | solution.py:369
  28.2 5.2 %collective-permute-start.8 = (bf16[2,64,1024]{2,1,0:T(8,128)(2,1)S(1)}, bf16[2,64,1024]{2,1,0:T(8,128)(2,1)S(1)}, u32[]{:S(2)}, u32[]{:S(2)}) collective-permute-start(bf16[2,64,1024]{2,1,0:T(8,128)(2,1)S(1)} %get-tuple-element.28), channel_id=1, source_target_pairs={{0,4},{4,0},{1,5},{5,1},{2,6},{6,2},{3,7},{7,3},{8,12},{12,8},{9,1... | collective-permute-start | bytes 786440 | tf_op jit(solution)/shard_map/ppermute | solution.py:365
  31.0 8.5 %collective-permute-start.12 = (bf16[64,1024]{1,0:T(8,128)(2,1)S(1)}, bf16[64,1024]{1,0:T(8,128)(2,1)S(1)}, u32[]{:S(2)}, u32[]{:S(2)}) collective-permute-start(bf16[64,1024]{1,0:T(8,128)(2,1)S(1)} %fold.4.refs_2_), channel_id=1, source_target_pairs={{0,2},{1,3},{2,0},{3,1},{4,6},{5,7},{6,4},{7,5},{8,10},{9,11},{10,... | collective-permute-start | bytes 393224 | tf_op jit(solution)/shard_map/ppermute | solution.py:369
  33.4 6.3 %collective-permute-start.11 = (bf16[64,1024]{1,0:T(8,128)(2,1)S(1)}, bf16[64,1024]{1,0:T(8,128)(2,1)S(1)}, u32[]{:S(2)}, u32[]{:S(2)}) collective-permute-start(bf16[64,1024]{1,0:T(8,128)(2,1)S(1)} %get-tuple-element.32), channel_id=1, source_target_pairs={{0,1},{1,0},{2,3},{3,2},{4,5},{5,4},{6,7},{7,6},{8,9},{9,8},{10,11... | collective-permute-start | bytes 393224 | tf_op jit(solution)/shard_map/ppermute | solution.py:369

commit v3 on v2

--- a/solution.py
+++ b/solution.py
@@ -134,19 +134,19 @@
         top = jnp.maximum(jnp.max(scores, axis=-1, keepdims=True), fresh)
         weights = jnp.exp2((scores - top) * factor)
         own_weight = jnp.exp2((fresh - top) * factor)
-        inverse = 1.0 / (jnp.sum(weights, axis=-1, keepdims=True) + own_weight)
-        own_weight = own_weight * inverse
         weights = weights.astype(jnp.bfloat16)
+        ones = jnp.ones((span, head), jnp.bfloat16)
         for g in range(groups):
             first = (h * groups + g) * span
             block_rows = slice(8 * heads * g, 8 * heads * (g + 1))
             attended = jnp.dot(
                 weights[block_rows], v_ref[first : first + span, :], preferred_element_type=jnp.float32
             )
-            attended = attended * inverse[block_rows]
+            total = jnp.dot(weights[block_rows], ones, preferred_element_type=jnp.float32) + own_weight[block_rows]
             own = slice(h * part + 8 * g, h * part + 8 * g + 8)
             fresh_values = vn_ref[h * part : (h + 1) * part, :].astype(jnp.float32)[8 * g : 8 * g + 8]
             attended = attended + own_weight[block_rows] * jnp.concatenate([fresh_values] * heads, axis=0)
+            attended = attended / total
             spread[g] = jnp.concatenate([attended[8 * i : 8 * i + 8] for i in range(heads)], axis=1)
         attended = jnp.concatenate(spread[:groups], axis=0)
         out_ref[stripe, :] = (res_ref[stripe, :].astype(jnp.float32) + attended).astype(out_ref.dtype)
@@ -175,7 +175,8 @@
 
 
 def silu_product(gate, up):
-    return (gate / (1.0 + jnp.exp(-gate)) * up).astype(jnp.bfloat16)
+    half = 0.5 * gate
+    return ((half + half * jnp.tanh(half)) * up).astype(jnp.bfloat16)
 
 
 def stage_kernel(devices, offsets, first, last, gain_ref, wg_ref, wu_ref, *refs):

time: 40.6 us -> 40.6 us (level)
  no operation moved by 1% of the time
where the time goes in v3:
time: 40.6 us; the launch traced here: 40.5 us
  starting transfers between devices  13.9 us (34%)
  waiting for transfers between devices  13.4 us (33%)
  Pallas kernels  11.6 us (29%)
  local copies, waits for them, and re-layouts  1.35 us (3%)
    ppermute x6, starting transfers between devices, exchange(): return lax.ppermute(x, 'dev', [(i, i ^ offset) for i in range(devices)])  12.1 us
    ppermute x6, waiting for transfers between devices, exchange(): return lax.ppermute(x, 'dev', [(i, i ^ offset) for i in range(devices)])  12 us
    pallas_call x3, Pallas kernels, stage(): pl.pallas_call(functools.partial(stage_kernel, devices, offsets, first, l...  5.09 us
    pallas_call x1, Pallas kernels, attend(): pl.pallas_call(functools.partial(attend_kernel, devices), out_shape=pltpu...  3 us
    pallas_call x3, Pallas kernels, down(): pl.pallas_call(functools.partial(down_kernel, devices, offsets), out_shap...  2.66 us
    ppermute x7, starting transfers between devices, swap(): return lax.ppermute(x, 'att', [(0, 1), (1, 0)])  1.85 us
    ppermute x7, waiting for transfers between devices, swap(): return lax.ppermute(x, 'att', [(0, 1), (1, 0)])  1.41 us
    unnamed x14, local copies, waits for them, and re-layouts  1.35 us
  transfers between devices with their start and end apart: 13, of which 8 were waited for; matrix products, arithmetic and copies ran while one was open for 0% of the time, Pallas kernels for 14%

profile of v3, /device:TPU:0, one launch (start us, length us, event | category | flops | bytes accessed | tf_op | source)
XLA Modules:
  0.0 40.5 jit_solution(7293540493225805494)
XLA Ops:
  0.0 3.0 %attend.1.refs_0_.stream_ref = bf16[64,1024]{1,0:T(8,128)(2,1)S(1)} custom-call(s32[1,2,32]{2,1,0:T(2,128)} %bitcast.16, bf16[64,1024]{1,0:T(8,128)(2,1)} %bitcast.12, bf16[4096,128]{1,0:T(8,128)(2,1)} %bitcast.10, bf16[4096,128]{1,0:T(8,128)(2,1)} %bitcast.11, bf16[64,128]{1,0:T(8,128)(2,1)} %bitcast.14, bf16[64,128]{1,0:T(8,128)(2,1)} %bitcast.15, ...), custom_call_target="tpu_custom_call" | custom-call | flops 60000002048 | tf_op jit(solution)/shard_map/attend/pallas_call | solution.py:159
  3.0 0.5 %collective-permute-start.2 = (bf16[64,1024]{1,0:T(8,128)(2,1)S(1)}, bf16[64,1024]{1,0:T(8,128)(2,1)S(1)}, u32[]{:S(2)}, u32[]{:S(2)}) collective-permute-start(bf16[64,1024]{1,0:T(8,128)(2,1)S(1)} %attend.1.refs_0_.stream_ref), channel_id=1, source_target_pairs={{0,4},{4,0},{1,5},{5,1},{2,6},{6,2},{3,7},{7,3},{8,12},{12,8},{9,1... | collective-permute-start | bytes 393224 | tf_op jit(solution)/shard_map/ppermute | solution.py:366
  3.5 3.7 %collective-permute-start = (bf16[64,1024]{1,0:T(8,128)(2,1)S(1)}, bf16[64,1024]{1,0:T(8,128)(2,1)S(1)}, u32[]{:S(2)}, u32[]{:S(2)}) collective-permute-start(bf16[64,1024]{1,0:T(8,128)(2,1)S(1)} %attend.1.refs_0_.stream_ref), channel_id=1, source_target_pairs={{0,2},{1,3},{2,0},{3,1},{4,6},{5,7},{6,4},{7,5},{8,10},{9,11},{10,... | collective-permute-start | bytes 393224 | tf_op jit(solution)/shard_map/ppermute | solution.py:370
  7.2 1.6 %collective-permute-start.4 = (bf16[64,1024]{1,0:T(8,128)(2,1)S(1)}, bf16[64,1024]{1,0:T(8,128)(2,1)S(1)}, u32[]{:S(2)}, u32[]{:S(2)}) collective-permute-start(bf16[64,1024]{1,0:T(8,128)(2,1)S(1)} %attend.1.refs_0_.stream_ref), channel_id=1, source_target_pairs={{0,1},{1,0},{2,3},{3,2},{4,5},{5,4},{6,7},{7,6},{8,9},{9,8},{10,11... | collective-permute-start | bytes 393224 | tf_op jit(solution)/shard_map/ppermute | solution.py:370
  8.8 0.0 collective-permute-done.2.refs_1_
  8.8 1.3 %copy-done.1 = bf16[4096,1792]{1,0:T(8,128)(2,1)S(1)} copy-done((bf16[4096,1792]{1,0:T(8,128)(2,1)S(1)}, bf16[4096,1792]{1,0:T(8,128)(2,1)}, u32[]{:S(2)}) %copy-start.1) | copy-done | bytes 14680088
  10.1 1.2 %stage.3 = (f32[128,1792]{1,0:T(8,128)S(1)}, f32[128,1792]{1,0:T(8,128)S(1)}, f32[128,128]{1,0:T(8,128)S(1)}) custom-call(bf16[4096]{0:T(1024)(128)(2,1)S(1)} %copy-done.2, bf16[4096,1792]{1,0:T(8,128)(2,1)S(1)} %copy-done, bf16[4096,1792]{1,0:T(8,128)(2,1)S(1)} %copy-done.1, bf16[64,1024]{1,0:T(8,128)(2,1)S(1)} %attend.1.refs_0_.stream_ref, ...), custom_call_target="tpu_custom_call" | custom-call | flops 1000000000 | tf_op jit(solution)/shard_map/stage/pallas_call | solution.py:267
  11.3 2.9 %collective-permute-done.piece_ref = bf16[64,1024]{1,0:T(8,128)(2,1)S(1)} collective-permute-done((bf16[64,1024]{1,0:T(8,128)(2,1)S(1)}, bf16[64,1024]{1,0:T(8,128)(2,1)S(1)}, u32[]{:S(2)}, u32[]{:S(2)}) %collective-permute-start) | collective-permute-done | bytes 131104 | tf_op jit(solution)/shard_map/ppermute | solution.py:370
  14.2 0.1 collective-permute-start.3
  14.3 0.1 collective-permute-done.4.piece_ref
  14.4 0.5 %collective-permute-start.5 = (bf16[64,1024]{1,0:T(8,128)(2,1)S(1)}, bf16[64,1024]{1,0:T(8,128)(2,1)S(1)}, u32[]{:S(2)}, u32[]{:S(2)}) collective-permute-start(bf16[64,1024]{1,0:T(8,128)(2,1)S(1)} %relay.4.refs_2_), channel_id=1, source_target_pairs={{0,4},{4,0},{1,5},{5,1},{2,6},{6,2},{3,7},{7,3},{8,12},{12,8},{9,1... | collective-permute-start | bytes 393224 | tf_op jit(solution)/shard_map/ppermute | solution.py:366
  14.9 1.2 %collective-permute-start.1 = (bf16[64,1024]{1,0:T(8,128)(2,1)S(1)}, bf16[64,1024]{1,0:T(8,128)(2,1)S(1)}, u32[]{:S(2)}, u32[]{:S(2)}) collective-permute-start(bf16[64,1024]{1,0:T(8,128)(2,1)S(1)} %collective-permute-done.piece_ref), channel_id=1, source_target_pairs={{0,1},{1,0},{2,3},{3,2},{4,5},{5,4},{6,7},{7,6},{8,9},{9,8},{10,11... | collective-permute-start | bytes 393224 | tf_op jit(solution)/shard_map/ppermute | solution.py:370
  16.1 0.0 slice-start.3
  16.1 2.5 %stage.4 = (f32[128,1792]{1,0:T(8,128)S(1)}, f32[128,1792]{1,0:T(8,128)S(1)}, f32[128,128]{1,0:T(8,128)S(1)}) custom-call(bf16[4096]{0:T(1024)(128)(2,1)S(1)} %copy-done.2, bf16[4096,1792]{1,0:T(8,128)(2,1)S(1)} %copy-done, bf16[4096,1792]{1,0:T(8,128)(2,1)S(1)} %copy-done.1, ...), custom_call_target="tpu_custom_call", output_to_operand_aliasing={{0}: (7, {}), {1}: (8, {}), {2}: (9, {})} | custom-call | flops 1000000000 | tf_op jit(solution)/shard_map/stage/pallas_call | solution.py:267
  18.6 1.8 %collective-permute-done.1.piece_ref = bf16[64,1024]{1,0:T(8,128)(2,1)S(1)} collective-permute-done((bf16[64,1024]{1,0:T(8,128)(2,1)S(1)}, bf16[64,1024]{1,0:T(8,128)(2,1)S(1)}, u32[]{:S(2)}, u32[]{:S(2)}) %collective-permute-start.1) | collective-permute-done | bytes 131104 | tf_op jit(solution)/shard_map/ppermute | solution.py:370
  20.4 0.1 collective-permute-start.6
  20.5 1.3 %collective-permute-done.6.refs_1_ = bf16[64,1024]{1,0:T(8,128)(2,1)S(1)} collective-permute-done((bf16[64,1024]{1,0:T(8,128)(2,1)S(1)}, bf16[64,1024]{1,0:T(8,128)(2,1)S(1)}, u32[]{:S(2)}, u32[]{:S(2)}) %collective-permute-start.6) | collective-permute-done | bytes 131104 | tf_op jit(solution)/shard_map/ppermute | solution.py:366
  21.8 1.4 %stage.5.hidden_ref = bf16[128,1792]{1,0:T(8,128)(2,1)S(1)} custom-call(bf16[4096]{0:T(1024)(128)(2,1)S(1)} %copy-done.2, bf16[4096,1792]{1,0:T(8,128)(2,1)S(1)} %copy-done, bf16[4096,1792]{1,0:T(8,128)(2,1)S(1)} %copy-done.1, bf16[64,1024]{1,0:T(8,128)(2,1)S(1)} %relay.5.refs_0_, bf16[64,1024]{1,0:T(8,128)(2,1)S(1)} %collective-permute-done.6.refs_1_, ...), custom_call_target="tpu_custom_call" | custom-call | flops 1000000000 | tf_op jit(solution)/shard_map/stage/pallas_call | solution.py:267
  23.2 0.7 %down.3 = (f32[1,64,1024]{2,1,0:T(8,128)S(1)}, bf16[1,64,1024]{2,1,0:T(8,128)(2,1)S(1)}) custom-call(bf16[128,1792]{1,0:T(8,128)(2,1)S(1)} %stage.5.hidden_ref, bf16[1792,4096]{1,0:T(8,128)(2,1)S(1)} %bitcast.9), custom_call_target="tpu_custom_call" | custom-call | flops 10000000000 | tf_op jit(solution)/shard_map/down/pallas_call | solution.py:314
  24.0 0.2 collective-permute-start.7
  24.2 0.7 %down.5 = (f32[1,64,1024]{2,1,0:T(8,128)S(1)}, bf16[1,64,1024]{2,1,0:T(8,128)(2,1)S(1)}) custom-call(bf16[128,1792]{1,0:T(8,128)(2,1)S(1)} %stage.5.hidden_ref, bf16[1792,4096]{1,0:T(8,128)(2,1)S(1)} %bitcast.9), custom_call_target="tpu_custom_call" | custom-call | flops 10000000000 | tf_op jit(solution)/shard_map/down/pallas_call | solution.py:314
  24.9 0.4 %collective-permute-start.9 = (bf16[1,64,1024]{2,1,0:T(8,128)(2,1)S(1)}, bf16[1,64,1024]{2,1,0:T(8,128)(2,1)S(1)}, u32[]{:S(2)}, u32[]{:S(2)}) collective-permute-start(bf16[1,64,1024]{2,1,0:T(8,128)(2,1)S(1)} %get-tuple-element.30), channel_id=1, source_target_pairs={{0,4},{4,0},{1,5},{5,1},{2,6},{6,2},{3,7},{7,3},{8,12},{12,8},{9,1... | collective-permute-start | bytes 393224 | tf_op jit(solution)/shard_map/ppermute | solution.py:366
  25.3 0.1 collective-permute-done.7.refs_1_
  25.4 1.6 %collective-permute-start.10 = (bf16[64,1024]{1,0:T(8,128)(2,1)S(1)}, bf16[64,1024]{1,0:T(8,128)(2,1)S(1)}, u32[]{:S(2)}, u32[]{:S(2)}) collective-permute-start(bf16[64,1024]{1,0:T(8,128)(2,1)S(1)} %fold.3.refs_0_), channel_id=1, source_target_pairs={{0,1},{1,0},{2,3},{3,2},{4,5},{5,4},{6,7},{7,6},{8,9},{9,8},{10,11... | collective-permute-start | bytes 393224 | tf_op jit(solution)/shard_map/ppermute | solution.py:370
  27.0 1.2 %down.4 = (f32[2,64,1024]{2,1,0:T(8,128)S(1)}, bf16[2,64,1024]{2,1,0:T(8,128)(2,1)S(1)}) custom-call(bf16[128,1792]{1,0:T(8,128)(2,1)S(1)} %stage.5.hidden_ref, bf16[1792,4096]{1,0:T(8,128)(2,1)S(1)} %bitcast.9, bf16[64,1024]{1,0:T(8,128)(2,1)S(1)} %fold.3.refs_0_), custom_call_target="tpu_custom_call" | custom-call | flops 10000000000 | tf_op jit(solution)/shard_map/down/pallas_call | solution.py:314
  28.2 0.1 collective-permute-start.8
  28.3 2.7 %collective-permute-done.10.refs_2_ = bf16[64,1024]{1,0:T(8,128)(2,1)S(1)} collective-permute-done((bf16[64,1024]{1,0:T(8,128)(2,1)S(1)}, bf16[64,1024]{1,0:T(8,128)(2,1)S(1)}, u32[]{:S(2)}, u32[]{:S(2)}) %collective-permute-start.10) | collective-permute-done | bytes 131104 | tf_op jit(solution)/shard_map/ppermute | solution.py:370
  31.1 2.3 %collective-permute-start.12 = (bf16[64,1024]{1,0:T(8,128)(2,1)S(1)}, bf16[64,1024]{1,0:T(8,128)(2,1)S(1)}, u32[]{:S(2)}, u32[]{:S(2)}) collective-permute-start(bf16[64,1024]{1,0:T(8,128)(2,1)S(1)} %fold.4.refs_2_), channel_id=1, source_target_pairs={{0,2},{1,3},{2,0},{3,1},{4,6},{5,7},{6,4},{7,5},{8,10},{9,11},{10,... | collective-permute-start | bytes 393224 | tf_op jit(solution)/shard_map/ppermute | solution.py:370
  33.4 1.8 %collective-permute-start.11 = (bf16[64,1024]{1,0:T(8,128)(2,1)S(1)}, bf16[64,1024]{1,0:T(8,128)(2,1)S(1)}, u32[]{:S(2)}, u32[]{:S(2)}) collective-permute-start(bf16[64,1024]{1,0:T(8,128)(2,1)S(1)} %get-tuple-element.32), channel_id=1, source_target_pairs={{0,1},{1,0},{2,3},{3,2},{4,5},{5,4},{6,7},{7,6},{8,9},{9,8},{10,11... | collective-permute-start | bytes 393224 | tf_op jit(solution)/shard_map/ppermute | solution.py:370
  35.2 4.4 %collective-permute-done.12.refs_2_ = bf16[64,1024]{1,0:T(8,128)(2,1)S(1)} collective-permute-done((bf16[64,1024]{1,0:T(8,128)(2,1)S(1)}, bf16[64,1024]{1,0:T(8,128)(2,1)S(1)}, u32[]{:S(2)}, u32[]{:S(2)}) %collective-permute-start.12) | collective-permute-done | bytes 131104 | tf_op jit(solution)/shard_map/ppermute | solution.py:370
  39.6 0.2 collective-permute-done.11.refs_1_
  39.8 0.7 %finish.1 = bf16[64,1024]{1,0:T(8,128)(2,1)} custom-call(bf16[64,1024]{1,0:T(8,128)(2,1)S(1)} %attend.1.refs_0_.stream_ref, f32[64,1024]{1,0:T(8,128)S(1)} %get-tuple-element.31.refs_0_, bf16[64,1024]{1,0:T(8,128)(2,1)S(1)} %collective-permute-done.11.refs_1_, bf16[64,1024]{1,0:T(8,128)(2,1)S(1)} %collective-permute-done.12.refs_2_), custom_call_target="tpu_custom_call" | custom-call | tf_op jit(solution)/shard_map/finish/pallas_call | solution.py:357
  (23 shorter events, 0.2 us)
Async XLA Ops:
  0.0 8.8 %copy-start = (bf16[4096,1792]{1,0:T(8,128)(2,1)S(1)}, bf16[4096,1792]{1,0:T(8,128)(2,1)}, u32[]{:S(2)}) copy-start(bf16[4096,1792]{1,0:T(8,128)(2,1)} %wg_ref.5) | copy-start | bytes 44040196
  0.0 10.1 %copy-start.1 = (bf16[4096,1792]{1,0:T(8,128)(2,1)S(1)}, bf16[4096,1792]{1,0:T(8,128)(2,1)}, u32[]{:S(2)}) copy-start(bf16[4096,1792]{1,0:T(8,128)(2,1)} %wu_ref.5) | copy-start | bytes 44040196
  0.0 10.1 %copy-start.2 = (bf16[4096]{0:T(1024)(128)(2,1)S(1)}, bf16[4096]{0:T(1024)(128)(2,1)}, u32[]{:S(2)}) copy-start(bf16[4096]{0:T(1024)(128)(2,1)} %gain_ref.5) | copy-start | bytes 24580
  3.0 5.8 %collective-permute-start.2 = (bf16[64,1024]{1,0:T(8,128)(2,1)S(1)}, bf16[64,1024]{1,0:T(8,128)(2,1)S(1)}, u32[]{:S(2)}, u32[]{:S(2)}) collective-permute-start(bf16[64,1024]{1,0:T(8,128)(2,1)S(1)} %attend.1.refs_0_.stream_ref), channel_id=1, source_target_pairs={{0,4},{4,0},{1,5},{5,1},{2,6},{6,2},{3,7},{7,3},{8,12},{12,8},{9,1... | collective-permute-start | bytes 393224 | tf_op jit(solution)/shard_map/ppermute | solution.py:366
  3.5 10.7 %collective-permute-start = (bf16[64,1024]{1,0:T(8,128)(2,1)S(1)}, bf16[64,1024]{1,0:T(8,128)(2,1)S(1)}, u32[]{:S(2)}, u32[]{:S(2)}) collective-permute-start(bf16[64,1024]{1,0:T(8,128)(2,1)S(1)} %attend.1.refs_0_.stream_ref), channel_id=1, source_target_pairs={{0,2},{1,3},{2,0},{3,1},{4,6},{5,7},{6,4},{7,5},{8,10},{9,11},{10,... | collective-permute-start | bytes 393224 | tf_op jit(solution)/shard_map/ppermute | solution.py:370
  7.2 7.2 %collective-permute-start.4 = (bf16[64,1024]{1,0:T(8,128)(2,1)S(1)}, bf16[64,1024]{1,0:T(8,128)(2,1)S(1)}, u32[]{:S(2)}, u32[]{:S(2)}) collective-permute-start(bf16[64,1024]{1,0:T(8,128)(2,1)S(1)} %attend.1.refs_0_.stream_ref), channel_id=1, source_target_pairs={{0,1},{1,0},{2,3},{3,2},{4,5},{5,4},{6,7},{7,6},{8,9},{9,8},{10,11... | collective-permute-start | bytes 393224 | tf_op jit(solution)/shard_map/ppermute | solution.py:370
  10.1 10.3 %slice-start = ((s8[14680064]{0:T(1024)(128)(4,1)}), s8[4194304]{0:T(1024)(128)(4,1)S(1)}, s32[]{:S(2)}) async-start(s8[14680064]{0:T(1024)(128)(4,1)} %bitcast.8), calls=%async_computation | async-start | bytes 8388608
  10.1 10.3 %slice-start.1 = ((s8[14680064]{0:T(1024)(128)(4,1)}), s8[4194304]{0:T(1024)(128)(4,1)S(1)}, s32[]{:S(2)}) async-start(s8[14680064]{0:T(1024)(128)(4,1)} %bitcast.8), calls=%async_computation.1 | async-start | bytes 8388608
  14.2 1.8 %collective-permute-start.3 = (bf16[64,1024]{1,0:T(8,128)(2,1)S(1)}, bf16[64,1024]{1,0:T(8,128)(2,1)S(1)}, u32[]{:S(2)}, u32[]{:S(2)}) collective-permute-start(bf16[64,1024]{1,0:T(8,128)(2,1)S(1)} %relay.3.refs_0_), channel_id=1, source_target_pairs={{0,4},{4,0},{1,5},{5,1},{2,6},{6,2},{3,7},{7,3},{8,12},{12,8},{9,1... | collective-permute-start | bytes 393224 | tf_op jit(solution)/shard_map/ppermute | solution.py:366
  14.4 1.7 %collective-permute-start.5 = (bf16[64,1024]{1,0:T(8,128)(2,1)S(1)}, bf16[64,1024]{1,0:T(8,128)(2,1)S(1)}, u32[]{:S(2)}, u32[]{:S(2)}) collective-permute-start(bf16[64,1024]{1,0:T(8,128)(2,1)S(1)} %relay.4.refs_2_), channel_id=1, source_target_pairs={{0,4},{4,0},{1,5},{5,1},{2,6},{6,2},{3,7},{7,3},{8,12},{12,8},{9,1... | collective-permute-start | bytes 393224 | tf_op jit(solution)/shard_map/ppermute | solution.py:366
  14.9 5.5 %collective-permute-start.1 = (bf16[64,1024]{1,0:T(8,128)(2,1)S(1)}, bf16[64,1024]{1,0:T(8,128)(2,1)S(1)}, u32[]{:S(2)}, u32[]{:S(2)}) collective-permute-start(bf16[64,1024]{1,0:T(8,128)(2,1)S(1)} %collective-permute-done.piece_ref), channel_id=1, source_target_pairs={{0,1},{1,0},{2,3},{3,2},{4,5},{5,4},{6,7},{7,6},{8,9},{9,8},{10,11... | collective-permute-start | bytes 393224 | tf_op jit(solution)/shard_map/ppermute | solution.py:370
  16.1 4.3 %slice-start.2 = ((s8[14680064]{0:T(1024)(128)(4,1)}), s8[4194304]{0:T(1024)(128)(4,1)S(1)}, s32[]{:S(2)}) async-start(s8[14680064]{0:T(1024)(128)(4,1)} %bitcast.8), calls=%async_computation.2 | async-start | bytes 8388608
  16.1 4.3 %slice-start.3 = ((s8[14680064]{0:T(1024)(128)(4,1)}), s8[2097152]{0:T(1024)(128)(4,1)S(1)}, s32[]{:S(2)}) async-start(s8[14680064]{0:T(1024)(128)(4,1)} %bitcast.8), calls=%async_computation.3 | async-start | bytes 4194304
  20.4 1.4 %collective-permute-start.6 = (bf16[64,1024]{1,0:T(8,128)(2,1)S(1)}, bf16[64,1024]{1,0:T(8,128)(2,1)S(1)}, u32[]{:S(2)}, u32[]{:S(2)}) collective-permute-start(bf16[64,1024]{1,0:T(8,128)(2,1)S(1)} %relay.5.refs_0_), channel_id=1, source_target_pairs={{0,4},{4,0},{1,5},{5,1},{2,6},{6,2},{3,7},{7,3},{8,12},{12,8},{9,1... | collective-permute-start | bytes 393224 | tf_op jit(solution)/shard_map/ppermute | solution.py:366
  24.0 1.4 %collective-permute-start.7 = (bf16[1,64,1024]{2,1,0:T(8,128)(2,1)S(1)}, bf16[1,64,1024]{2,1,0:T(8,128)(2,1)S(1)}, u32[]{:S(2)}, u32[]{:S(2)}) collective-permute-start(bf16[1,64,1024]{2,1,0:T(8,128)(2,1)S(1)} %get-tuple-element.26), channel_id=1, source_target_pairs={{0,4},{4,0},{1,5},{5,1},{2,6},{6,2},{3,7},{7,3},{8,12},{12,8},{9,1... | collective-permute-start | bytes 393224 | tf_op jit(solution)/shard_map/ppermute | solution.py:366
  24.9 3.4 %collective-permute-start.9 = (bf16[1,64,1024]{2,1,0:T(8,128)(2,1)S(1)}, bf16[1,64,1024]{2,1,0:T(8,128)(2,1)S(1)}, u32[]{:S(2)}, u32[]{:S(2)}) collective-permute-start(bf16[1,64,1024]{2,1,0:T(8,128)(2,1)S(1)} %get-tuple-element.30), channel_id=1, source_target_pairs={{0,4},{4,0},{1,5},{5,1},{2,6},{6,2},{3,7},{7,3},{8,12},{12,8},{9,1... | collective-permute-start | bytes 393224 | tf_op jit(solution)/shard_map/ppermute | solution.py:366
  25.4 5.6 %collective-permute-start.10 = (bf16[64,1024]{1,0:T(8,128)(2,1)S(1)}, bf16[64,1024]{1,0:T(8,128)(2,1)S(1)}, u32[]{:S(2)}, u32[]{:S(2)}) collective-permute-start(bf16[64,1024]{1,0:T(8,128)(2,1)S(1)} %fold.3.refs_0_), channel_id=1, source_target_pairs={{0,1},{1,0},{2,3},{3,2},{4,5},{5,4},{6,7},{7,6},{8,9},{9,8},{10,11... | collective-permute-start | bytes 393224 | tf_op jit(solution)/shard_map/ppermute | solution.py:370
  28.2 5.1 %collective-permute-start.8 = (bf16[2,64,1024]{2,1,0:T(8,128)(2,1)S(1)}, bf16[2,64,1024]{2,1,0:T(8,128)(2,1)S(1)}, u32[]{:S(2)}, u32[]{:S(2)}) collective-permute-start(bf16[2,64,1024]{2,1,0:T(8,128)(2,1)S(1)} %get-tuple-element.28), channel_id=1, source_target_pairs={{0,4},{4,0},{1,5},{5,1},{2,6},{6,2},{3,7},{7,3},{8,12},{12,8},{9,1... | collective-permute-start | bytes 786440 | tf_op jit(solution)/shard_map/ppermute | solution.py:366
  31.1 8.5 %collective-permute-start.12 = (bf16[64,1024]{1,0:T(8,128)(2,1)S(1)}, bf16[64,1024]{1,0:T(8,128)(2,1)S(1)}, u32[]{:S(2)}, u32[]{:S(2)}) collective-permute-start(bf16[64,1024]{1,0:T(8,128)(2,1)S(1)} %fold.4.refs_2_), channel_id=1, source_target_pairs={{0,2},{1,3},{2,0},{3,1},{4,6},{5,7},{6,4},{7,5},{8,10},{9,11},{10,... | collective-permute-start | bytes 393224 | tf_op jit(solution)/shard_map/ppermute | solution.py:370
  33.4 6.4 %collective-permute-start.11 = (bf16[64,1024]{1,0:T(8,128)(2,1)S(1)}, bf16[64,1024]{1,0:T(8,128)(2,1)S(1)}, u32[]{:S(2)}, u32[]{:S(2)}) collective-permute-start(bf16[64,1024]{1,0:T(8,128)(2,1)S(1)} %get-tuple-element.32), channel_id=1, source_target_pairs={{0,1},{1,0},{2,3},{3,2},{4,5},{5,4},{6,7},{7,6},{8,9},{9,8},{10,11... | collective-permute-start | bytes 393224 | tf_op jit(solution)/shard_map/ppermute | solution.py:370
